TPU v7x, 256 devices: a whole 4x4x8 slice. The times are simulated.
256 devices in a mesh: layer: 4 (over x), prow: 8 (over z), pcol: 8 (over y, core).
Axes of the slice: x: 4, y: 4, z: 8, core: 2. Of those that a mesh axis runs over, the one named last changes fastest.
Arguments:
- separator: float32 [8192, 8192], P('prow', 'pcol'), may hold values from -6 to 6
- left_factor: bfloat16 [16384, 128, 128], P(('layer', 'prow', 'pcol')), may hold values from -6 to 6
- right_factor: bfloat16 [16384, 128, 128], P(('layer', 'prow', 'pcol')), may hold values from -0.5 to 0.5
- owners: int32 [16384, 1], P(('layer', 'prow', 'pcol')), may hold values from 0 to 63; in each aligned block of 64 rows (0 to 63, 64 to 127, ...) at most 2 rows name the same one
- spots: int32 [16384], P(('layer', 'prow', 'pcol')), may hold values from 0 to 63
- pivot_order: int32 [512], replicated, may hold values from 0 to 511, each once
- panel_inverses: bfloat16 [512, 512], replicated, may hold values from -0.2 to 0.2
Outputs:
- factored: float32 [8192, 8192], P('prow', 'pcol')
Inputs may be any that keep to these rules, and one draw needn't show every extreme that they name: `owners`: of the 64 update blocks of one device, at most 2 name the same owner.
All inputs are finite; a program needn't handle non-finite values.
Results may differ from a plain program's by a relative error of at most 0.0003.
Values sent between devices are 32-bit elements; how exact they have to be, the bound alone decides.
A program may use at most 128 MiB of HBM per device.

v0:
```python
import jax
import jax.numpy as jnp
from jax import lax
from jax.sharding import PartitionSpec as P


def broadcast(x, axis, root):
    mine = lax.axis_index(axis) == root
    return lax.psum(jnp.where(mine, x, jnp.zeros_like(x)), axis)


def per_device(separator, left_factor, right_factor, owners, spots, pivot_order, panel_inverses):
    panel_width = pivot_order.shape[0]
    update_count = left_factor.shape[0]
    block_size = left_factor.shape[1]
    grid_rows = lax.axis_size("prow")
    grid_cols = lax.axis_size("pcol")
    owner_count = grid_rows * grid_cols
    capacity = 2 * update_count // owner_count
    slots_total = owner_count * capacity
    piece_rows, piece_cols = separator.shape
    per_row = piece_rows // block_size
    per_col = piece_cols // block_size
    square = block_size * block_size
    products = jnp.einsum(
        "uab,ubc->uac", left_factor, right_factor, preferred_element_type=jnp.float32
    )
    destination = owners[:, 0]
    chosen = (destination[:, None] == jnp.arange(owner_count)[None, :]).astype(jnp.float32)
    strict_lower = jnp.tril(jnp.ones((update_count, update_count), jnp.float32), -1)
    earlier = jnp.dot(strict_lower, chosen, precision=lax.Precision.HIGHEST)
    slot_rank = jnp.sum(earlier * chosen, axis=1).astype(jnp.int32)
    slot_index = destination * capacity + slot_rank
    dispatch = jnp.arange(slots_total)[:, None] == slot_index[None, :]
    outgoing = jnp.dot(
        dispatch.astype(jnp.float32),
        products.reshape(update_count, square),
        precision=lax.Precision.HIGHEST,
    )
    outgoing_spots = jnp.sum(jnp.where(dispatch, spots[None, :], 0), axis=1)
    arrived, arrived_spots = (
        lax.all_to_all(outgoing, ("prow", "pcol"), split_axis=0, concat_axis=0, tiled=True),
        lax.all_to_all(outgoing_spots, ("prow", "pcol"), split_axis=0, concat_axis=0, tiled=True),
    )
    placing = (arrived_spots[:, None] == jnp.arange(per_row * per_col)[None, :]).astype(jnp.float32)
    gathered = jnp.einsum("rp,rq->pq", placing, arrived, precision=lax.Precision.HIGHEST)
    local_sum = (
        gathered.reshape(per_row, per_col, block_size, block_size)
        .transpose(0, 2, 1, 3)
        .reshape(piece_rows, piece_cols)
    )
    reduced = separator - lax.psum(local_sum, "layer")
    top_rows = jnp.take(reduced[:panel_width], pivot_order, axis=0)
    left_block = reduced[:, :panel_width]
    inverses = panel_inverses.astype(jnp.float32)
    lower_inverse = jnp.tril(inverses, -1) + jnp.eye(panel_width, dtype=jnp.float32)
    upper_inverse = jnp.triu(inverses)
    upper_rows = broadcast(top_rows, "prow", 0)
    left_columns = broadcast(left_block, "pcol", 0)
    upper_part = jnp.dot(lower_inverse, upper_rows, precision=lax.Precision.HIGHEST)
    lower_part = jnp.dot(left_columns, upper_inverse, precision=lax.Precision.HIGHEST)
    trailing = reduced - jnp.dot(lower_part, upper_part, precision=lax.Precision.HIGHEST)
    row_global = lax.axis_index("prow") * piece_rows + jnp.arange(piece_rows)
    col_global = lax.axis_index("pcol") * piece_cols + jnp.arange(piece_cols)
    panel_cols = col_global < panel_width
    panel_rows = row_global < panel_width
    widened_lower = jnp.pad(lower_part, ((0, 0), (0, piece_cols - panel_width)))
    body_rows = jnp.where(panel_cols[None, :], widened_lower, trailing)
    head_rows = jnp.where(panel_cols[None, :], top_rows, upper_part)
    head_full = jnp.pad(head_rows, ((0, piece_rows - panel_width), (0, 0)))
    return jnp.where(panel_rows[:, None], head_full, body_rows)


def solution(mesh):
    in_specs = (
        P("prow", "pcol"),
        P(("layer", "prow", "pcol"), None, None),
        P(("layer", "prow", "pcol"), None, None),
        P(("layer", "prow", "pcol"), None),
        P(("layer", "prow", "pcol")),
        P(),
        P(),
    )
    out_specs = P("prow", "pcol")
    return jax.shard_map(
        per_device, mesh=mesh, in_specs=in_specs, out_specs=out_specs, check_vma=False
    )
```

profile of v0, /device:TPU:144, one launch (start us, length us, event | category | flops | bytes accessed | tf_op | source)
XLA Modules:
  0.0 546.1 jit_solution(10809107543745186997)
XLA Ops:
  6.5 0.0 copy-start
  6.5 1.0 fusion
  7.5 0.7 convert_add_fusion
  8.2 0.7 select_reduce_fusion
  8.9 0.7 all_to_all.12
  9.7 10.3 %all-to-all-start = ((s32[64,2,1]{1,2,0:T(1,128)}), s32[64,2,1]{1,2,0:T(1,128)S(1)}, u32[]{:S(2)}, u32[]{:S(2)}) async-start(s32[64,2,1]{1,2,0:T(1,128)} %bitcast.1), calls=%async_computation | async-start | bytes 65536 | tf_op jit(solution)/shard_map/all_to_all | solution.py:43
  20.0 0.0 copy-done
  20.0 4.3 fusion.28
  24.3 4.9 reshape.86
  29.3 5.3 fusion.10
  34.6 7.8 %copy.14 = f32[64,2,16384]{2,1,0:T(2,128)} copy(f32[64,2,16384]{2,0,1:T(8,128)S(1)} %fusion.10) | data formatting | bytes 16777216 | tf_op jit(solution)/shard_map/dot_general | solution.py:35
  42.4 0.0 all-to-all-done
  42.4 10.5 %all-to-all-start.1 = ((f32[64,2,16384]{2,1,0:T(2,128)}), f32[64,2,16384]{2,1,0:T(2,128)}, u32[]{:S(2)}, u32[]{:S(2)}) async-start(f32[64,2,16384]{2,1,0:T(2,128)} %copy.14), calls=%async_computation.1 | async-start | bytes 16777216 | tf_op jit(solution)/shard_map/all_to_all | solution.py:42
  52.9 0.0 all-reduce.6.cloned.1.call-start
  53.0 0.5 broadcast.84
  53.5 0.7 reduce.3
  54.2 0.1 eq.89
  54.4 179.0 %all-to-all-done.1 = f32[64,2,16384]{2,1,0:T(2,128)} async-done(((f32[64,2,16384]{2,1,0:T(2,128)}), f32[64,2,16384]{2,1,0:T(2,128)}, u32[]{:S(2)}, u32[]{:S(2)}) %all-to-all-start.1) | async-done | bytes 8388640 | tf_op jit(solution)/shard_map/all_to_all | solution.py:42
  233.4 10.9 %all_to_all.15 = f32[128,16384]{1,0:T(8,128)} reshape(f32[64,2,16384]{2,1,0:T(2,128)} %all-to-all-done.1) | data formatting | bytes 16777216 | tf_op jit(solution)/shard_map/all_to_all | solution.py:42
  244.2 9.0 %copy.15 = f32[16384,128]{1,0:T(8,128)} copy(f32[16384,128]{0,1:T(8,128)} %bitcast.28) | data formatting | bytes 16777216 | tf_op jit(solution)/shard_map/rp,rq->pq/dot_general | solution.py:46
  253.2 7.4 %fusion.15 = f32[8,8,128,128]{3,1,2,0:T(8,128)S(1)} fusion(f32[128,128,128,1]{2,1,0,3:T(8,128)} %bitcast.27, s32[8,8]{1,0:T(8,128)S(1)} %multiply_add_fusion, s32[128]{0:T(128)S(1)} %eq.89), kind=kOutput, calls=%fused_computation.29 | convolution fusion | flops 1610620928 | bytes 12583680 | tf_op jit(solution)/shard_map/rp,rq->pq/dot_general | solution.py:46
  260.6 3.0 copy.19
  263.6 0.0 all-reduce.6.cloned.1.call-update
  263.7 0.0 all-reduce.10.cloned.1.call-start
  263.7 101.0 %all-reduce.6.cloned.1.call-done = f32[1024,1024]{1,0:T(8,128)} async-done(((f32[1024,1024]{1,0:T(8,128)}), f32[1024,1024]{1,0:T(8,128)}) %all-reduce.6.cloned.1.call-update) | async-done | bytes 4194320 | tf_op jit(solution)/shard_map/psum | solution.py:52
  364.7 4.4 sub.6
  369.1 0.0 copy-start.2
  369.1 2.0 copy-done.2
  371.1 1.6 slice_select_fusion
  372.7 0.0 copy-start.7
  372.7 0.0 all-reduce.10.cloned.1.call-update
  372.7 0.2 all-reduce.8.cloned.1.call-start
  373.0 0.4 copy-done.7
  373.4 0.0 slice-start
  373.4 1.6 slice-done
  375.0 2.7 gather_fusion
  377.7 3.2 select_select_fusion.2
  380.9 0.0 copy-start.6
  380.9 0.0 all-reduce.8.cloned.1.call-update
  381.0 0.0 copy-start.4
  381.0 58.5 %all-reduce.10.cloned.1.call-done = f32[1024,512]{1,0:T(8,128)} async-done(((f32[1024,512]{1,0:T(8,128)}), f32[1024,512]{1,0:T(8,128)}) %all-reduce.10.cloned.1.call-update) | async-done | bytes 2097168 | tf_op jit(solution)/shard_map/psum | solution.py:9
  439.5 0.0 copy-done.6
  439.5 6.7 %fusion.4 = f32[1024,512]{1,0:T(8,128)} fusion(f32[1024,512]{1,0:T(8,128)} %all-reduce.10.cloned.1.call-done, bf16[512,512]{1,0:T(8,128)(2,1)S(1)} %copy-done.6, s32[512]{0:T(512)S(1)} %iota_add_fusion), kind=kOutput, calls=%fused_computation.12 | convolution fusion | flops 3222011904 | bytes 4720640 | tf_op jit(solution)/shard_map/dot_general | solution.py:61
  446.2 79.0 %all-reduce.8.cloned.1.call-done = f32[512,1024]{1,0:T(8,128)} async-done(((f32[512,1024]{1,0:T(8,128)}), f32[512,1024]{1,0:T(8,128)}) %all-reduce.8.cloned.1.call-update) | async-done | bytes 2097168 | tf_op jit(solution)/shard_map/psum | solution.py:9
  525.2 0.0 copy-done.4
  525.2 0.0 copy-start.3
  525.2 0.0 copy-start.5
  525.2 5.6 %select_select_fusion.1 = (f32[512,1024]{1,0:T(8,128)S(1)}, f32[512,1024]{1,0:T(8,128)S(1)}) fusion(f32[512,1024]{1,0:T(8,128)S(1)} %copy-done.4, pred[512]{0:T(512)(128)(4,1)S(1)} %compare_and_fusion, pred[1024]{0:T(1024)(128)(4,1)S(1)} %get-tuple-element.7, f32[512,1024]{1,0:T(8,128)} %all-reduce.8.cloned.1.call-done, bf16[512,512]{1,0:T(8,128)(2,1)S(1)} %copy-done.6, ...), kind=kOutput, calls=%fused_computation.4 | convolution fusion | flops 3223846912 | bytes 8916480 | tf_op jit(solution)/shard_map/dot_general | solution.py:60
  530.8 0.0 copy-done.3
  530.8 0.0 copy-done.5
  530.8 0.0 copy-start.1
  530.8 8.7 %select_select_fusion = f32[1024,1024]{1,0:T(8,128)} fusion(f32[1024,1024]{1,0:T(8,128)S(1)} %copy-done.3, f32[1024,512]{1,0:T(8,128)S(1)} %copy-done.5, f32[512,1024]{1,0:T(8,128)S(1)} %get-tuple-element.5, f32[512,1024]{1,0:T(8,128)S(1)} %get-tuple-element.6, pred[1024]{0:T(1024)(128)(4,1)S(1)} %get-tuple-element.8, pred[1024]{0:T(1024)(128)(4,1)S(1)} %get-tuple-element.7), kind=kOutput, calls=%fused_computation.2 | convolution fusion | flops 6445596672 | bytes 14682112 | tf_op jit(solution)/shard_map/dot_general | solution.py:62
  539.6 0.0 copy-done.1
  (8 shorter events, 0.0 us)
Async XLA Ops:
  6.5 13.5 %copy-start = (bf16[64,128,128]{2,1,0:T(8,128)(2,1)S(1)}, bf16[64,128,128]{2,1,0:T(8,128)(2,1)}, u32[]{:S(2)}) copy-start(bf16[64,128,128]{2,1,0:T(8,128)(2,1)} %param.8) | copy-start | bytes 6291460
  9.7 32.7 %all-to-all-start = ((s32[64,2,1]{1,2,0:T(1,128)}), s32[64,2,1]{1,2,0:T(1,128)S(1)}, u32[]{:S(2)}, u32[]{:S(2)}) async-start(s32[64,2,1]{1,2,0:T(1,128)} %bitcast.1), calls=%async_computation | async-start | bytes 65536 | tf_op jit(solution)/shard_map/all_to_all | solution.py:43
  42.4 191.0 %all-to-all-start.1 = ((f32[64,2,16384]{2,1,0:T(2,128)}), f32[64,2,16384]{2,1,0:T(2,128)}, u32[]{:S(2)}, u32[]{:S(2)}) async-start(f32[64,2,16384]{2,1,0:T(2,128)} %copy.14), calls=%async_computation.1 | async-start | bytes 16777216 | tf_op jit(solution)/shard_map/all_to_all | solution.py:42
  52.9 311.8 %all-reduce.6.cloned.1.call-start = ((), (), s32[]{:S(2)}) async-start(), calls=%async_computation.2 | async-start | bytes 8388608 | tf_op jit(solution)/shard_map/psum | solution.py:52
  263.7 175.9 %all-reduce.10.cloned.1.call-start = ((), (), s32[]{:S(2)}) async-start(), calls=%async_computation.4 | async-start | bytes 4194304 | tf_op jit(solution)/shard_map/psum | solution.py:9
  369.1 2.0 copy-start.2
  372.7 0.7 copy-start.7
  372.7 152.5 %all-reduce.8.cloned.1.call-start = ((), (), s32[]{:S(2)}) async-start(), calls=%async_computation.3 | async-start | bytes 4194304 | tf_op jit(solution)/shard_map/psum | solution.py:9
  373.4 1.6 slice-start
  380.9 58.6 %copy-start.6 = (bf16[512,512]{1,0:T(8,128)(2,1)S(1)}, bf16[512,512]{1,0:T(8,128)(2,1)}, u32[]{:S(2)}) copy-start(bf16[512,512]{1,0:T(8,128)(2,1)} %param.13) | copy-start | bytes 1572868
  381.0 144.2 %copy-start.4 = (f32[512,1024]{1,0:T(8,128)S(1)}, f32[512,1024]{1,0:T(8,128)}, u32[]{:S(2)}) copy-start(f32[512,1024]{1,0:T(8,128)} %gather_fusion) | copy-start | bytes 6291460
  525.2 5.6 %copy-start.3 = (f32[1024,1024]{1,0:T(8,128)S(1)}, f32[1024,1024]{1,0:T(8,128)}, u32[]{:S(2)}) copy-start(f32[1024,1024]{1,0:T(8,128)} %copy-done.2) | copy-start | bytes 12582916
  525.2 5.6 %copy-start.5 = (f32[1024,512]{1,0:T(8,128)S(1)}, f32[1024,512]{1,0:T(8,128)}, u32[]{:S(2)}) copy-start(f32[1024,512]{1,0:T(8,128)} %fusion.4) | copy-start | bytes 6291460
  530.8 8.7 %copy-start.1 = (bf16[64,128,128]{2,1,0:T(8,128)(2,1)S(1)}, bf16[64,128,128]{2,1,0:T(8,128)(2,1)}, u32[]{:S(2)}) copy-start(bf16[64,128,128]{2,1,0:T(8,128)(2,1)} %param.8) | copy-start | bytes 6291460
Sparse Core Ops, SparseCore 0:
  263.8 100.8 all-reduce.5
  372.9 66.6 all-reduce.9
  442.0 83.1 all-reduce.7
where the time goes:
time: 551 us; the launch traced here: 546 us
  waiting for transfers between devices  418 us (76%)
  local copies, waits for them, and re-layouts  43.8 us (8%)
  matrix products  38.9 us (7%)
  starting transfers between devices  21.1 us (4%)
  between operations  13.3 us (2%)
  other arithmetic  11.4 us (2%)
    all_to_all x1, waiting for transfers between devices, per_device(): lax.all_to_all(outgoing, ('prow', 'pcol'), split_axis=0, concat_axis=0, t...  179 us
    psum x2, waiting for transfers between devices, broadcast(): return lax.psum(jnp.where(mine, x, jnp.zeros_like(x)), axis)  138 us
    psum x1, waiting for transfers between devices, per_device(): reduced = separator - lax.psum(local_sum, 'layer')  101 us
  transfers between devices with their start and end apart: 5, of which 4 were waited for; matrix products, arithmetic and copies ran while one was open for 7% of the time, Pallas kernels for 0%

commit v1 on v0

v1 whole, which is shorter than its diff:
```python
import functools

import jax
import jax.numpy as jnp
from jax import lax
from jax.experimental import pallas as pl
from jax.experimental.pallas import tpu as pltpu
from jax.sharding import PartitionSpec as P

MESH = pl.DeviceIdType.MESH
GRID = 8
OWNERS = GRID * GRID
BLOCK = 128
F32 = jnp.float32


def broadcast(x, axis, root):
    mine = lax.axis_index(axis) == root
    return lax.psum(jnp.where(mine, x, jnp.zeros_like(x)), axis)


def exchange_kernel(index_ref, left_ref, right_ref, recv_ref, out_buf, send_sem, recv_sem, own_sem):
    layer, row, col = lax.axis_index("layer"), lax.axis_index("prow"), lax.axis_index("pcol")
    me = row * GRID + col

    def place(k):
        r = (row + k % GRID) % GRID
        c = (col + k // GRID) % GRID
        return r, c

    barrier = pltpu.get_barrier_semaphore()

    def greet(k, carry):
        r, c = place(k)
        pl.semaphore_signal(barrier, inc=1, device_id=(layer, r, c), device_id_type=MESH)
        return carry

    lax.fori_loop(1, OWNERS, greet, 0)

    def product(k):
        r, c = place(k)
        u = index_ref[r * GRID + c]
        out_buf[k] = jnp.dot(left_ref[u], right_ref[u], preferred_element_type=F32)

    def copy(k):
        r, c = place(k)
        return pltpu.make_async_remote_copy(
            src_ref=out_buf.at[k],
            dst_ref=recv_ref.at[me],
            send_sem=send_sem.at[k],
            recv_sem=recv_sem.at[k],
            device_id=(layer, r, c),
            device_id_type=MESH,
        )

    pl.semaphore_wait(barrier, OWNERS - 1)

    def send(k, carry):
        product(k)
        copy(k).start()
        return carry

    lax.fori_loop(1, OWNERS, send, 0)
    product(0)
    own = pltpu.make_async_copy(out_buf.at[0], recv_ref.at[me], own_sem)
    own.start()
    own.wait()

    def finish(k, carry):
        copy(k).wait()
        return carry

    lax.fori_loop(1, OWNERS, finish, 0)


def exchange(index, left, right):
    return pl.pallas_call(
        exchange_kernel,
        out_shape=jax.ShapeDtypeStruct((OWNERS, BLOCK, BLOCK), F32),
        in_specs=[
            pl.BlockSpec(memory_space=pltpu.SMEM),
            pl.BlockSpec(memory_space=pltpu.VMEM),
            pl.BlockSpec(memory_space=pltpu.VMEM),
        ],
        out_specs=pl.BlockSpec(memory_space=pl.ANY),
        scratch_shapes=[
            pltpu.VMEM((OWNERS, BLOCK, BLOCK), F32),
            pltpu.SemaphoreType.DMA((OWNERS,)),
            pltpu.SemaphoreType.DMA((OWNERS,)),
            pltpu.SemaphoreType.DMA,
        ],
        compiler_params=pltpu.CompilerParams(
            collective_id=0, has_side_effects=True, vmem_limit_bytes=32 * 1024 * 1024
        ),
        cost_estimate=pl.CostEstimate(
            flops=2 * OWNERS * BLOCK**3, bytes_accessed=16 * 1024 * 1024, transcendentals=0
        ),
    )(index, left, right)


def scatter_kernel(per_step, spot_ref, extra_ref, recv_ref, extra_hbm, out_ref, extra_buf, extra_sem):
    step = pl.program_id(0)

    @pl.when(step == 0)
    def _():
        out_ref[...] = jnp.zeros_like(out_ref)

    def add(k, carry):
        spot = spot_ref[step * per_step + k]

        @pl.when(spot < 64)
        def _():
            slot = (spot % 8) * 8 + spot // 8
            out_ref[slot] += recv_ref[k]

        return carry

    lax.fori_loop(0, per_step, add, 0)

    def add_extra(k, carry):
        spot = extra_ref[step * per_step + k]

        @pl.when(spot < 64)
        def _():
            fetch = pltpu.make_async_copy(extra_hbm.at[step * per_step + k], extra_buf, extra_sem)
            fetch.start()
            fetch.wait()
            slot = (spot % 8) * 8 + spot // 8
            out_ref[slot] += extra_buf[...]

        return carry

    lax.fori_loop(0, per_step, add_extra, 0)


def scatter(spots, extra_spots, recv, extra):
    per_step = 8
    return pl.pallas_call(
        functools.partial(scatter_kernel, per_step),
        out_shape=jax.ShapeDtypeStruct((64, BLOCK, BLOCK), F32),
        grid=(OWNERS // per_step,),
        in_specs=[
            pl.BlockSpec(memory_space=pltpu.SMEM),
            pl.BlockSpec(memory_space=pltpu.SMEM),
            pl.BlockSpec((per_step, BLOCK, BLOCK), lambda i: (i, 0, 0)),
            pl.BlockSpec(memory_space=pl.ANY),
        ],
        out_specs=pl.BlockSpec((64, BLOCK, BLOCK), lambda i: (0, 0, 0)),
        scratch_shapes=[pltpu.VMEM((BLOCK, BLOCK), F32), pltpu.SemaphoreType.DMA],
        compiler_params=pltpu.CompilerParams(vmem_limit_bytes=24 * 1024 * 1024),
    )(spots, extra_spots, recv, extra)


def scatter_extra_kernel(extra_ref, dense_ref, extra_ref_data, out_ref):
    out_ref[...] = dense_ref[...]

    def add(k, carry):
        spot = extra_ref[k]

        @pl.when(spot < 64)
        def _():
            slot = (spot % 8) * 8 + spot // 8
            out_ref[slot] += extra_ref_data[k]

        return carry

    lax.fori_loop(0, OWNERS, add, 0)


def scatter_extra(extra_spots, dense, extra):
    return pl.pallas_call(
        scatter_extra_kernel,
        out_shape=jax.ShapeDtypeStruct((64, BLOCK, BLOCK), F32),
        in_specs=[
            pl.BlockSpec(memory_space=pltpu.SMEM),
            pl.BlockSpec(memory_space=pltpu.VMEM),
            pl.BlockSpec(memory_space=pltpu.VMEM),
        ],
        out_specs=pl.BlockSpec(memory_space=pltpu.VMEM),
        compiler_params=pltpu.CompilerParams(vmem_limit_bytes=24 * 1024 * 1024),
    )(extra_spots, dense, extra)


def local_sum(left, right, owners, spots):
    update_count = left.shape[0]
    most = update_count // 2
    destination = owners[:, 0]
    counter = jnp.arange(update_count)
    same = destination[:, None] == destination[None, :]
    rank = jnp.sum(same & (counter[None, :] < counter[:, None]), axis=1)
    named = (destination[None, :] == jnp.arange(OWNERS)[:, None]) & (rank == 0)[None, :]
    index = jnp.sum(jnp.where(named, counter[None, :], 0), axis=1)
    first_spot = jnp.sum(jnp.where(named, spots[None, :], 0), axis=1)
    first_spot = jnp.where(jnp.any(named, axis=1), first_spot, 64)
    second = rank == 1
    order = jnp.sum(second[None, :] & (counter[None, :] < counter[:, None]), axis=1)
    picked = second[None, :] & (order[None, :] == jnp.arange(most)[:, None])
    extra_index = jnp.sum(jnp.where(picked, counter[None, :], 0), axis=1)
    extra_code = jnp.sum(jnp.where(picked, destination[None, :] * 64 + spots[None, :], 0), axis=1)
    extra_code = jnp.where(jnp.any(picked, axis=1), extra_code, -1)
    table = jnp.concatenate([first_spot, extra_code, jnp.zeros((32,), jnp.int32)])[None, :]
    table = lax.all_gather(table, ("layer", "prow", "pcol"), axis=0, tiled=True)
    me = lax.axis_index("prow") * GRID + lax.axis_index("pcol")
    layer_table = lax.dynamic_slice_in_dim(table, lax.axis_index("layer") * OWNERS, OWNERS, 0)
    my_spots = lax.dynamic_index_in_dim(layer_table, me, 1, keepdims=False)
    rounds = jnp.max(jnp.sum(table[:, OWNERS : OWNERS + most] >= 0, axis=1))

    def extra_round(k):
        u = extra_index[k]
        block = jnp.dot(left[u], right[u], preferred_element_type=F32)
        blocks = lax.all_gather(block[None], ("prow", "pcol"), axis=0, tiled=True)
        code = lax.dynamic_index_in_dim(layer_table, OWNERS + k, 1, keepdims=False)
        extra_spots = jnp.where((code >= 0) & (code // 64 == me), code % 64, 64)
        return extra_spots, blocks

    recv = exchange(index, left, right)
    extra_spots, blocks = extra_round(0)
    dense = scatter(my_spots, extra_spots, recv, blocks)

    def body(carry):
        k, dense = carry
        extra_spots, blocks = extra_round(k)
        return k + 1, scatter_extra(extra_spots, dense, blocks)

    return lax.while_loop(lambda carry: carry[0] < rounds, body, (jnp.int32(1), dense))[1]


def per_device(separator, left_factor, right_factor, owners, spots, pivot_order, panel_inverses):
    panel_width = pivot_order.shape[0]
    piece_rows, piece_cols = separator.shape
    dense = local_sum(left_factor, right_factor, owners, spots)
    dense = dense.reshape(8, piece_rows, BLOCK).transpose(1, 0, 2).reshape(piece_rows, piece_cols)
    reduced = separator - lax.psum(dense, "layer")
    top_rows = jnp.take(reduced[:panel_width], pivot_order, axis=0)
    left_block = reduced[:, :panel_width]
    inverses = panel_inverses.astype(jnp.float32)
    lower_inverse = jnp.tril(inverses, -1) + jnp.eye(panel_width, dtype=jnp.float32)
    upper_inverse = jnp.triu(inverses)
    upper_rows = broadcast(top_rows, "prow", 0)
    left_columns = broadcast(left_block, "pcol", 0)
    upper_part = jnp.dot(lower_inverse, upper_rows, precision=lax.Precision.HIGHEST)
    lower_part = jnp.dot(left_columns, upper_inverse, precision=lax.Precision.HIGHEST)
    trailing = reduced - jnp.dot(lower_part, upper_part, precision=lax.Precision.HIGHEST)
    row_global = lax.axis_index("prow") * piece_rows + jnp.arange(piece_rows)
    col_global = lax.axis_index("pcol") * piece_cols + jnp.arange(piece_cols)
    panel_cols = col_global < panel_width
    panel_rows = row_global < panel_width
    widened_lower = jnp.pad(lower_part, ((0, 0), (0, piece_cols - panel_width)))
    body_rows = jnp.where(panel_cols[None, :], widened_lower, trailing)
    head_rows = jnp.where(panel_cols[None, :], top_rows, upper_part)
    head_full = jnp.pad(head_rows, ((0, piece_rows - panel_width), (0, 0)))
    return jnp.where(panel_rows[:, None], head_full, body_rows)


def solution(mesh):
    in_specs = (
        P("prow", "pcol"),
        P(("layer", "prow", "pcol"), None, None),
        P(("layer", "prow", "pcol"), None, None),
        P(("layer", "prow", "pcol"), None),
        P(("layer", "prow", "pcol")),
        P(),
        P(),
    )
    return jax.shard_map(
        per_device, mesh=mesh, in_specs=in_specs, out_specs=P("prow", "pcol"), check_vma=False
    )
```

time: 551 us -> 482 us (0.87)
  waiting for transfers between devices: 418 us -> 237 us
  Pallas kernels: 0 us -> 113 us
  blocking collectives: 0 us -> 54.5 us
  local copies, waits for them, and re-layouts: 43.8 us -> 22.3 us
  starting transfers between devices: 21.1 us -> 0.31 us
  matrix products: 38.9 us -> 22.5 us
    all_to_all x2 -> x0, waiting for transfers between devices: 179 us -> none  [the longest x1 179 us: per_device(): lax.all_to_all(outgoing, ('prow', 'pcol'), split_axis=0, concat_axis=0, t...]
    pallas_call x0 -> x2, Pallas kernels: none -> 113 us  [the longest x1 107 us: exchange(): pl.pallas_call(exchange_kernel, out_shape=jax.ShapeDtypeStruct((OWNERS, B...]
    all_gather x0 -> x1, blocking collectives: none -> 54.5 us  [local_sum(): table = lax.all_gather(table, ('layer', 'prow', 'pcol'), axis=0, tiled=True)]
    all_to_all x2 -> x0, starting transfers between devices: 20.8 us -> none  [the longest x1 10.5 us: per_device(): lax.all_to_all(outgoing, ('prow', 'pcol'), split_axis=0, concat_axis=0, t...]
    dot_general x2 -> x0, local copies, waits for them, and re-layouts: 16.8 us -> none  [the longest x1 9.01 us: per_device(): jnp.einsum('rp,rq->pq', placing, arrived, precision=lax.Precision.HIGHEST)]
    dot_general x4 -> x1, matrix products: 18 us -> 1.55 us  [extra_round(): block = jnp.dot(left[u], right[u], preferred_element_type=F32)]
    all_to_all x3 -> x0, local copies, waits for them, and re-layouts: 12.1 us -> none  [the longest x1 10.9 us: per_device(): lax.all_to_all(outgoing, ('prow', 'pcol'), split_axis=0, concat_axis=0, t...]
    unnamed x17 -> x19, local copies, waits for them, and re-layouts: 5.47 us -> 11.8 us
  transfers between devices with their start and end apart: 5 -> 4, of which waited for: 4 -> 3; matrix products, arithmetic and copies ran while one was open for 7% -> 3% of each run, Pallas kernels for 0% -> 22%
where the time goes in v1:
time: 482 us; the launch traced here: 478 us
  waiting for transfers between devices  237 us (49%)
  Pallas kernels  113 us (23%)
  blocking collectives  54.5 us (11%)
  matrix products  22.5 us (5%)
  local copies, waits for them, and re-layouts  22.3 us (5%)
  other arithmetic  13.7 us (3%)
  between operations  13.5 us (3%)
    psum x2, waiting for transfers between devices, broadcast(): return lax.psum(jnp.where(mine, x, jnp.zeros_like(x)), axis)  137 us
    pallas_call x1, Pallas kernels, exchange(): pl.pallas_call(exchange_kernel, out_shape=jax.ShapeDtypeStruct((OWNERS, B...  107 us
    psum x1, waiting for transfers between devices, per_device(): reduced = separator - lax.psum(dense, 'layer')  100 us
    all_gather x1, blocking collectives, local_sum(): table = lax.all_gather(table, ('layer', 'prow', 'pcol'), axis=0, tiled=True)  54.5 us
    unnamed x19, local copies, waits for them, and re-layouts  11.8 us
  transfers between devices with their start and end apart: 4, of which 3 were waited for; matrix products, arithmetic and copies ran while one was open for 3% of the time, Pallas kernels for 22%

profile of v1, /device:TPU:144, one launch (start us, length us, event | category | flops | bytes accessed | tf_op | source)
XLA Modules:
  0.0 477.9 jit_solution(4727376241134059379)
XLA Ops:
  6.5 0.0 all-gather.9.cloned.1.call-start
  6.5 0.9 convert_reduce_fusion.2
  7.4 0.7 multiply_add_fusion
  8.1 0.8 select_reduce_fusion
  9.0 0.1 select_reduce_fusion.2
  9.2 1.5 fusion.16
  10.8 0.0 all-gather.9.cloned.1.call-update
  10.8 0.1 fusion.26
  10.9 0.8 fusion.24
  11.7 0.1 add_bitcast_fusion
  11.8 54.5 %all-gather.3 = s32[256,1,128]{2,1,0:T(1,128)S(1)} all-gather(s32[1,1,128]{2,1,0:T(1,128)S(1)} %add_bitcast_fusion), channel_id=3, replica_groups=mesh['layer'=4,'prow'=8,'pcol'=8] {'layer','prow','pcol'}, dimensions={0}, use_global_device_ids=true | all-gather | bytes 131584 | tf_op jit(solution)/shard_map/all_gather | solution.py:202
  66.3 0.1 copy.17
  66.4 0.2 convert_reduce_fusion
  66.6 0.7 reduce_max.9
  67.3 1.3 dynamic-slice_reduce_fusion.spot_ref
  68.6 107.4 %shard_map.73.recv_ref = f32[64,128,128]{2,1,0:T(8,128)S(1)} custom-call(s32[64]{0:T(128)S(1)} %get-tuple-element.146.index_ref, bf16[64,128,128]{2,1,0:T(8,128)(2,1)} %left_ref.1, bf16[64,128,128]{2,1,0:T(8,128)(2,1)} %right_ref.1), custom_call_target="tpu_custom_call" | custom-call | flops 268435456 | bytes 16777216 | tf_op jit(solution)/shard_map/pallas_call | solution.py:77
  176.0 0.0 copy-start.2
  176.0 2.0 copy-done.2
  178.0 0.2 slice_reduce_fusion
  178.2 0.0 all-gather.9.cloned.1.call-done
  178.3 0.0 copy-start.3
  178.3 2.2 copy-done.3
  180.5 0.0 copy-start.4
  180.5 2.2 copy-done.4
  182.6 5.5 %shard_map.74 = f32[64,128,128]{2,1,0:T(8,128)} custom-call(s32[64]{0:T(128)S(1)} %dynamic-slice_reduce_fusion.spot_ref, s32[64]{0:T(128)S(1)} %and_select_fusion.4.extra_ref, f32[64,128,128]{2,1,0:T(8,128)S(1)} %copy-done.3, f32[64,128,128]{2,1,0:T(8,128)S(1)} %bitcast.50), custom_call_target="tpu_custom_call" | custom-call | tf_op jit(solution)/shard_map/pallas_call | solution.py:138
  188.2 0.7 while.12
  188.9 0.0 all-reduce.6.cloned.1.call-start
  188.9 4.6 copy.18
  193.6 3.0 copy.21
  196.6 0.0 all-reduce.6.cloned.1.call-update
  196.6 0.0 all-reduce.10.cloned.1.call-start
  196.7 100.0 %all-reduce.6.cloned.1.call-done = f32[1024,1024]{1,0:T(8,128)} async-done(((f32[1024,1024]{1,0:T(8,128)}), f32[1024,1024]{1,0:T(8,128)}) %all-reduce.6.cloned.1.call-update) | async-done | bytes 4194320 | tf_op jit(solution)/shard_map/psum | solution.py:233
  296.7 4.4 sub.19
  301.1 0.0 copy-start.5
  301.1 2.0 copy-done.5
  303.1 1.6 slice_select_fusion
  304.7 0.0 copy-start.10
  304.7 0.0 all-reduce.10.cloned.1.call-update
  304.7 0.2 all-reduce.8.cloned.1.call-start
  304.9 0.4 copy-done.10
  305.4 0.0 slice-start
  305.4 1.6 slice-done
  307.0 2.7 gather_fusion
  309.7 3.2 select_select_fusion.2
  312.9 0.0 copy-start.9
  312.9 0.0 all-reduce.8.cloned.1.call-update
  313.0 0.0 copy-start.7
  313.0 58.5 %all-reduce.10.cloned.1.call-done = f32[1024,512]{1,0:T(8,128)} async-done(((f32[1024,512]{1,0:T(8,128)}), f32[1024,512]{1,0:T(8,128)}) %all-reduce.10.cloned.1.call-update) | async-done | bytes 2097168 | tf_op jit(solution)/shard_map/psum | solution.py:19
  371.5 0.0 copy-done.9
  371.5 6.6 %fusion.10 = f32[1024,512]{1,0:T(8,128)} fusion(f32[1024,512]{1,0:T(8,128)} %all-reduce.10.cloned.1.call-done, bf16[512,512]{1,0:T(8,128)(2,1)S(1)} %copy-done.9, s32[512]{0:T(512)S(1)} %iota_add_fusion), kind=kOutput, calls=%fused_computation.24 | convolution fusion | flops 3222011904 | bytes 4720640 | tf_op jit(solution)/shard_map/dot_general | solution.py:242
  378.1 78.9 %all-reduce.8.cloned.1.call-done = f32[512,1024]{1,0:T(8,128)} async-done(((f32[512,1024]{1,0:T(8,128)}), f32[512,1024]{1,0:T(8,128)}) %all-reduce.8.cloned.1.call-update) | async-done | bytes 2097168 | tf_op jit(solution)/shard_map/psum | solution.py:19
  457.0 0.0 copy-done.7
  457.0 0.0 copy-start.6
  457.0 0.0 copy-start.8
  457.0 5.6 %select_select_fusion.1 = (f32[512,1024]{1,0:T(8,128)S(1)}, f32[512,1024]{1,0:T(8,128)S(1)}) fusion(f32[512,1024]{1,0:T(8,128)S(1)} %copy-done.7, pred[512]{0:T(512)(128)(4,1)S(1)} %compare_and_fusion, pred[1024]{0:T(1024)(128)(4,1)S(1)} %get-tuple-element.169, f32[512,1024]{1,0:T(8,128)} %all-reduce.8.cloned.1.call-done, ...), kind=kOutput, calls=%fused_computation.18 | convolution fusion | flops 3223846912 | bytes 8916480 | tf_op jit(solution)/shard_map/dot_general | solution.py:241
  462.6 0.0 copy-done.6
  462.6 0.0 copy-done.8
  462.6 8.7 %select_select_fusion = f32[1024,1024]{1,0:T(8,128)} fusion(f32[1024,1024]{1,0:T(8,128)S(1)} %copy-done.6, f32[1024,512]{1,0:T(8,128)S(1)} %copy-done.8, f32[512,1024]{1,0:T(8,128)S(1)} %get-tuple-element.166, f32[512,1024]{1,0:T(8,128)S(1)} %get-tuple-element.167, pred[1024]{0:T(1024)(128)(4,1)S(1)} %get-tuple-element.170, ...), kind=kOutput, calls=%fused_computation.16 | convolution fusion | flops 6445596672 | bytes 14682112 | tf_op jit(solution)/shard_map/dot_general | solution.py:243
  (11 shorter events, 0.1 us)
Async XLA Ops:
  6.5 171.7 %all-gather.9.cloned.1.call-start = ((), (), s32[]{:S(2)}) async-start(), calls=%async_computation.3 | async-start | bytes 4259840 | tf_op jit(solution)/shard_map/all_gather | solution.py:211
  176.0 2.0 copy-start.2
  178.3 2.2 copy-start.3
  180.5 2.2 copy-start.4
  188.9 107.8 %all-reduce.6.cloned.1.call-start = ((), (), s32[]{:S(2)}) async-start(), calls=%async_computation | async-start | bytes 8388608 | tf_op jit(solution)/shard_map/psum | solution.py:233
  196.6 174.9 %all-reduce.10.cloned.1.call-start = ((), (), s32[]{:S(2)}) async-start(), calls=%async_computation.2 | async-start | bytes 4194304 | tf_op jit(solution)/shard_map/psum | solution.py:19
  301.1 2.0 copy-start.5
  304.7 0.7 copy-start.10
  304.7 152.3 %all-reduce.8.cloned.1.call-start = ((), (), s32[]{:S(2)}) async-start(), calls=%async_computation.1 | async-start | bytes 4194304 | tf_op jit(solution)/shard_map/psum | solution.py:19
  305.4 1.6 slice-start
  312.9 58.6 %copy-start.9 = (bf16[512,512]{1,0:T(8,128)(2,1)S(1)}, bf16[512,512]{1,0:T(8,128)(2,1)}, u32[]{:S(2)}) copy-start(bf16[512,512]{1,0:T(8,128)(2,1)} %param.15) | copy-start | bytes 1572868
  313.0 144.0 %copy-start.7 = (f32[512,1024]{1,0:T(8,128)S(1)}, f32[512,1024]{1,0:T(8,128)}, u32[]{:S(2)}) copy-start(f32[512,1024]{1,0:T(8,128)} %gather_fusion) | copy-start | bytes 6291460
  457.0 5.6 %copy-start.6 = (f32[1024,1024]{1,0:T(8,128)S(1)}, f32[1024,1024]{1,0:T(8,128)}, u32[]{:S(2)}) copy-start(f32[1024,1024]{1,0:T(8,128)} %copy-done.5) | copy-start | bytes 12582916
  457.0 5.6 %copy-start.8 = (f32[1024,512]{1,0:T(8,128)S(1)}, f32[1024,512]{1,0:T(8,128)}, u32[]{:S(2)}) copy-start(f32[1024,512]{1,0:T(8,128)} %fusion.10) | copy-start | bytes 6291460
Sparse Core Ops, SparseCore 0:
  10.9 84.3 all-gather.8
  196.7 99.9 all-reduce.5
  304.8 66.6 all-reduce.9
  373.8 83.1 all-reduce.7

commit v2 on v1

--- a/solution.py
+++ b/solution.py
@@ -9,17 +9,16 @@
 
 MESH = pl.DeviceIdType.MESH
 GRID = 8
+LAYERS = 4
 OWNERS = GRID * GRID
 BLOCK = 128
 F32 = jnp.float32
 
 
-def broadcast(x, axis, root):
-    mine = lax.axis_index(axis) == root
-    return lax.psum(jnp.where(mine, x, jnp.zeros_like(x)), axis)
-
-
-def exchange_kernel(index_ref, left_ref, right_ref, recv_ref, out_buf, send_sem, recv_sem, own_sem):
+def exchange_kernel(
+    index_ref, table_ref, left_ref, right_ref, recv_ref, tables_ref, peak_ref,
+    out_buf, table_buf, peak_buf, send_sem, recv_sem, own_sem, table_send, table_recv, peak_send, peak_recv,
+):
     layer, row, col = lax.axis_index("layer"), lax.axis_index("prow"), lax.axis_index("pcol")
     me = row * GRID + col
 
@@ -28,6 +27,9 @@
         c = (col + k // GRID) % GRID
         return r, c
 
+    def other(k):
+        return ((layer + k) % LAYERS, row, col)
+
     barrier = pltpu.get_barrier_semaphore()
 
     def greet(k, carry):
@@ -36,6 +38,8 @@
         return carry
 
     lax.fori_loop(1, OWNERS, greet, 0)
+    for k in range(1, LAYERS):
+        pl.semaphore_signal(barrier, inc=1, device_id=other(k), device_id_type=MESH)
 
     def product(k):
         r, c = place(k)
@@ -53,17 +57,56 @@
             device_id_type=MESH,
         )
 
-    pl.semaphore_wait(barrier, OWNERS - 1)
+    def table_copy(k):
+        r, c = place(k)
+        return pltpu.make_async_remote_copy(
+            src_ref=table_ref,
+            dst_ref=table_buf.at[me],
+            send_sem=table_send.at[k],
+            recv_sem=table_recv.at[k],
+            device_id=(layer, r, c),
+            device_id_type=MESH,
+        )
+
+    def peak_copy(k):
+        return pltpu.make_async_remote_copy(
+            src_ref=peak_buf.at[0],
+            dst_ref=peak_buf.at[k],
+            send_sem=peak_send.at[k],
+            recv_sem=peak_recv.at[k],
+            device_id=other(k),
+            device_id_type=MESH,
+        )
+
+    product(0)
+    product(1)
+    pl.semaphore_wait(barrier, OWNERS - 1 + LAYERS - 1)
+
+    def send_table(k, carry):
+        table_copy(k).start()
+        return carry
 
     def send(k, carry):
-        product(k)
         copy(k).start()
-        return carry
-
-    lax.fori_loop(1, OWNERS, send, 0)
-    product(0)
+        product(k + 1)
+        return carry
+
+    lax.fori_loop(1, OWNERS - 1, send, 0)
+    copy(OWNERS - 1).start()
+    lax.fori_loop(1, OWNERS, send_table, 0)
     own = pltpu.make_async_copy(out_buf.at[0], recv_ref.at[me], own_sem)
     own.start()
+    table_buf[me] = table_ref[...]
+
+    def finish_table(k, carry):
+        table_copy(k).wait()
+        return carry
+
+    lax.fori_loop(1, OWNERS, finish_table, 0)
+    tables_ref[...] = table_buf[...]
+    peak_buf[0] = jnp.max(table_buf[...], axis=0)
+    for k in range(1, LAYERS):
+        peak_copy(k).start()
     own.wait()
 
     def finish(k, carry):
@@ -71,23 +114,33 @@
         return carry
 
     lax.fori_loop(1, OWNERS, finish, 0)
-
-
-def exchange(index, left, right):
+    for k in range(1, LAYERS):
+        peak_copy(k).wait()
+    peak_ref[...] = jnp.max(peak_buf[...], axis=0)
+
+
+def exchange(index, table, left, right):
+    vmem = pl.BlockSpec(memory_space=pltpu.VMEM)
     return pl.pallas_call(
         exchange_kernel,
-        out_shape=jax.ShapeDtypeStruct((OWNERS, BLOCK, BLOCK), F32),
-        in_specs=[
-            pl.BlockSpec(memory_space=pltpu.SMEM),
-            pl.BlockSpec(memory_space=pltpu.VMEM),
-            pl.BlockSpec(memory_space=pltpu.VMEM),
-        ],
-        out_specs=pl.BlockSpec(memory_space=pl.ANY),
+        out_shape=(
+            jax.ShapeDtypeStruct((OWNERS, BLOCK, BLOCK), F32),
+            jax.ShapeDtypeStruct((OWNERS, 8, BLOCK), jnp.int32),
+            jax.ShapeDtypeStruct((8, BLOCK), jnp.int32),
+        ),
+        in_specs=[pl.BlockSpec(memory_space=pltpu.SMEM), vmem, vmem, vmem],
+        out_specs=(pl.BlockSpec(memory_space=pl.ANY), vmem, vmem),
         scratch_shapes=[
             pltpu.VMEM((OWNERS, BLOCK, BLOCK), F32),
+            pltpu.VMEM((OWNERS, 8, BLOCK), jnp.int32),
+            pltpu.VMEM((LAYERS, 8, BLOCK), jnp.int32),
             pltpu.SemaphoreType.DMA((OWNERS,)),
             pltpu.SemaphoreType.DMA((OWNERS,)),
             pltpu.SemaphoreType.DMA,
+            pltpu.SemaphoreType.DMA((OWNERS,)),
+            pltpu.SemaphoreType.DMA((OWNERS,)),
+            pltpu.SemaphoreType.DMA((LAYERS,)),
+            pltpu.SemaphoreType.DMA((LAYERS,)),
         ],
         compiler_params=pltpu.CompilerParams(
             collective_id=0, has_side_effects=True, vmem_limit_bytes=32 * 1024 * 1024
@@ -95,7 +148,7 @@
         cost_estimate=pl.CostEstimate(
             flops=2 * OWNERS * BLOCK**3, bytes_accessed=16 * 1024 * 1024, transcendentals=0
         ),
-    )(index, left, right)
+    )(index, table, left, right)
 
 
 def scatter_kernel(per_step, spot_ref, extra_ref, recv_ref, extra_hbm, out_ref, extra_buf, extra_sem):
@@ -110,8 +163,7 @@
 
         @pl.when(spot < 64)
         def _():
-            slot = (spot % 8) * 8 + spot // 8
-            out_ref[slot] += recv_ref[k]
+            out_ref[spot] += recv_ref[k]
 
         return carry
 
@@ -125,8 +177,7 @@
             fetch = pltpu.make_async_copy(extra_hbm.at[step * per_step + k], extra_buf, extra_sem)
             fetch.start()
             fetch.wait()
-            slot = (spot % 8) * 8 + spot // 8
-            out_ref[slot] += extra_buf[...]
+            out_ref[spot] += extra_buf[...]
 
         return carry
 
@@ -159,8 +210,7 @@
 
         @pl.when(spot < 64)
         def _():
-            slot = (spot % 8) * 8 + spot // 8
-            out_ref[slot] += extra_ref_data[k]
+            out_ref[spot] += extra_ref_data[k]
 
         return carry
 
@@ -198,12 +248,16 @@
     extra_index = jnp.sum(jnp.where(picked, counter[None, :], 0), axis=1)
     extra_code = jnp.sum(jnp.where(picked, destination[None, :] * 64 + spots[None, :], 0), axis=1)
     extra_code = jnp.where(jnp.any(picked, axis=1), extra_code, -1)
-    table = jnp.concatenate([first_spot, extra_code, jnp.zeros((32,), jnp.int32)])[None, :]
-    table = lax.all_gather(table, ("layer", "prow", "pcol"), axis=0, tiled=True)
-    me = lax.axis_index("prow") * GRID + lax.axis_index("pcol")
-    layer_table = lax.dynamic_slice_in_dim(table, lax.axis_index("layer") * OWNERS, OWNERS, 0)
-    my_spots = lax.dynamic_index_in_dim(layer_table, me, 1, keepdims=False)
-    rounds = jnp.max(jnp.sum(table[:, OWNERS : OWNERS + most] >= 0, axis=1))
+    count = jnp.sum(second).astype(jnp.int32)
+    table = jnp.concatenate([first_spot, extra_code, jnp.full((32,), count)]).astype(jnp.int32)
+    table = jnp.broadcast_to(table[None, :], (8, 128))
+    col = lax.axis_index("pcol")
+    me = lax.axis_index("prow") * GRID + col
+
+    def slot_of(spot):
+        i, j = spot // 8, spot % 8
+        inside = jnp.where(j < 4, (i // 2) * 16 + j * 2 + i % 2, (2 * (j - 4) + 1) * 8 + i)
+        return jnp.where(spot < 64, jnp.where(col == 0, inside, j * 8 + i), 64)
 
     def extra_round(k):
         u = extra_index[k]
@@ -211,9 +265,12 @@
         blocks = lax.all_gather(block[None], ("prow", "pcol"), axis=0, tiled=True)
         code = lax.dynamic_index_in_dim(layer_table, OWNERS + k, 1, keepdims=False)
         extra_spots = jnp.where((code >= 0) & (code // 64 == me), code % 64, 64)
-        return extra_spots, blocks
-
-    recv = exchange(index, left, right)
+        return slot_of(extra_spots), blocks
+
+    recv, tables, peak = exchange(index, table, left, right)
+    layer_table = tables[:, 0, :]
+    rounds = peak[0, 96]
+    my_spots = slot_of(lax.dynamic_index_in_dim(layer_table, me, 1, keepdims=False))
     extra_spots, blocks = extra_round(0)
     dense = scatter(my_spots, extra_spots, recv, blocks)
 
@@ -225,31 +282,426 @@
     return lax.while_loop(lambda carry: carry[0] < rounds, body, (jnp.int32(1), dense))[1]
 
 
+def split(x):
+    high = x.astype(jnp.bfloat16)
+    return high, (x - high.astype(F32)).astype(jnp.bfloat16)
+
+
+def dot(a, b):
+    return jnp.dot(a, b, preferred_element_type=F32)
+
+
+def panel_kernel(
+    dense_ref, sep_ref, inv_ref, pivot_ref, out_ref,
+    sep_buf, relay, comb, plain, red, top, left, low, up_hi, up_lo, up, perm, inv_lp, inv_u,
+    sep_sem, rs_send, rs_recv, top_send, top_recv, ly_send, ly_recv, lx_send, lx_recv, lc_send, lc_recv,
+    ag_send, ag_recv, fw_send, fw_recv, out_sem,
+):
+    layer, row, col = lax.axis_index("layer"), lax.axis_index("prow"), lax.axis_index("pcol")
+    core = col % 2
+    nxt, prv, opp = (layer + 1) % LAYERS, (layer + 3) % LAYERS, (layer + 2) % LAYERS
+    edge = col == 0
+    head = row == 0
+    half = 4 * BLOCK
+
+    def remote(src, dst, send, recv, device):
+        return pltpu.make_async_remote_copy(
+            src_ref=src, dst_ref=dst, send_sem=send, recv_sem=recv, device_id=device, device_id_type=MESH
+        )
+
+    to_nxt, to_prv, to_opp = (nxt, row, col), (prv, row, col), (opp, row, col)
+    up_row, down_row = (row + 1) % GRID, (row + GRID - 1) % GRID
+
+    barrier = pltpu.get_barrier_semaphore()
+    for device in (to_nxt, to_prv, to_opp, (layer, up_row, col), (layer, down_row, col)):
+        pl.semaphore_signal(barrier, inc=1, device_id=device, device_id_type=MESH)
+    for k in range(1, GRID):
+        pl.semaphore_signal(barrier, inc=1, device_id=(layer, row, (col + k) % GRID), device_id_type=MESH)
+
+    def sep_first():
+        return pltpu.make_async_copy(
+            sep_ref.at[:, pl.ds(pl.multiple_of(layer * 2 * BLOCK, BLOCK), BLOCK)], sep_buf.at[0], sep_sem.at[0]
+        )
+
+    def sep_edge(j):
+        return pltpu.make_async_copy(
+            sep_ref.at[pl.ds(pl.multiple_of(layer * 256, 256), 256), pl.ds(j * BLOCK, BLOCK)],
+            sep_buf.at[0, pl.ds(j * 256, 256)],
+            sep_sem.at[2 + j],
+        )
+
+    def column(q, h):
+        normal = 2 * q + h
+        return pl.multiple_of(jnp.where(edge, 4 + q, normal) * BLOCK, BLOCK)
+
+    sep_second = pltpu.make_async_copy(
+        sep_ref.at[:, pl.ds(column(layer, 1), BLOCK)], sep_buf.at[1], sep_sem.at[1]
+    )
+    sep_second.start()
+
+    @pl.when(jnp.logical_not(edge))
+    def _():
+        sep_first().start()
+
+    @pl.when(edge)
+    def _():
+        for j in range(4):
+            sep_edge(j).start()
+
+    pl.semaphore_wait(barrier, 5 + GRID - 1)
+
+    relay_out = [
+        remote(dense_ref.at[2 * opp], relay.at[0], rs_send.at[0], rs_recv.at[0], to_nxt),
+        remote(dense_ref.at[2 * opp + 1], relay.at[1], rs_send.at[1], rs_recv.at[1], to_prv),
+    ]
+    plain_out = [
+        remote(dense_ref.at[2 * prv], plain.at[0], rs_send.at[2], rs_recv.at[2], to_prv),
+        remote(dense_ref.at[2 * nxt + 1], plain.at[1], rs_send.at[3], rs_recv.at[3], to_nxt),
+    ]
+    comb_out = [
+        remote(relay.at[0], comb.at[0], rs_send.at[4], rs_recv.at[4], to_nxt),
+        remote(relay.at[1], comb.at[1], rs_send.at[5], rs_recv.at[5], to_prv),
+    ]
+    relay_out[0].start()
+    relay_out[1].start()
+    plain_out[1].start()
+    plain_out[0].start()
+
+    inv = inv_ref[...]
+    rows_at = lax.broadcasted_iota(jnp.int32, (half, half), 0)
+    cols_at = lax.broadcasted_iota(jnp.int32, (half, half), 1)
+    inv_f = inv.astype(F32)
+    lower_inverse = jnp.where(rows_at > cols_at, inv_f, jnp.where(rows_at == cols_at, 1.0, 0.0))
+    inv_u[...] = jnp.where(rows_at <= cols_at, inv_f, 0.0).astype(jnp.bfloat16)
+    perm[...] = jnp.where(pivot_ref[...] == cols_at, 1.0, 0.0).astype(jnp.bfloat16)
+    inv_lp[...] = dot(lower_inverse.astype(jnp.bfloat16), perm[...]).astype(jnp.bfloat16)
+
+    relay_out[0].wait_recv()
+    relay[0] += dense_ref[2 * nxt]
+    comb_out[0].start()
+    relay_out[1].wait_recv()
+    relay[1] += dense_ref[2 * prv + 1]
+    comb_out[1].start()
+
+    @pl.when(jnp.logical_not(edge))
+    def _():
+        sep_first().wait()
+
+    @pl.when(edge)
+    def _():
+        for j in range(4):
+            sep_edge(j).wait()
+
+    sep_second.wait()
+    for h in range(2):
+        plain_out[h].wait_recv()
+        red[h] = sep_buf[h] - (dense_ref[2 * layer + h] + plain[h])
+    for h in range(2):
+        comb_out[h].wait_recv()
+        red[h] -= comb[h]
+
+    def top_copy(h, s, d):
+        part = top.at[h, pl.ds(s * 256, 256)]
+        return remote(
+            part, part, top_send.at[d, h, s], top_recv.at[h, s],
+            (layer, (up_row if d == 0 else down_row), col),
+        )
+
+    def top_wait(h, s):
+        top_copy(h, s, 0).wait_recv()
+
+    onward = jnp.logical_and(row >= 1, row <= 3)
+    backward = row >= 6
+
+    def for_top(action):
+        for h in (1, 0):
+            for s in range(2):
+                if h == 1:
+                    action(h, s)
+                else:
+                    pl.when(jnp.logical_not(edge))(functools.partial(action, h, s))
+
+    @pl.when(head)
+    def _():
+        top[0] = red[0, :half]
+        top[1] = red[1, :half]
+
+        def action(h, s):
+            top_copy(h, s, 0).start()
+            top_copy(h, s, 1).start()
+
+        for_top(action)
+
+    @pl.when(jnp.logical_and(edge, jnp.logical_not(head)))
+    def _():
+        top[0] = jnp.zeros((half, BLOCK), F32)
+
+    def left_y(k):
+        c = (col + k) % GRID
+        part = left.at[layer, pl.ds((c % 2) * half, half)]
+        return remote(part, part, ly_send.at[k], ly_recv, (layer, row, c))
+
+    @pl.when(edge)
+    def _():
+        left[layer] = red[0]
+        for k in (2, 3, 6, 7, 4, 5, 1):
+            left_y(k).start()
+
+    @pl.when(jnp.logical_not(edge))
+    def _():
+        mine = left.at[layer, pl.ds(core * half, half)]
+        remote(mine, mine, ly_send.at[0], ly_recv, (layer, row, (col + 1) % GRID)).wait_recv()
+
+    def left_x(k):
+        part = left.at[layer, pl.ds(core * half, half)]
+        return remote(part, part, lx_send.at[k], lx_recv.at[k], ((layer + k) % LAYERS, row, col))
+
+    def left_x_wait(k):
+        part = left.at[(layer + LAYERS - k) % LAYERS, pl.ds(core * half, half)]
+        remote(part, part, lx_send.at[k], lx_recv.at[k], ((layer + k) % LAYERS, row, col)).wait_recv()
+
+    sibling = (layer, row, col + 1 - 2 * core)
+
+    def left_c(k):
+        part = left.at[(layer + k) % LAYERS, pl.ds(core * half, half)]
+        return remote(part, part, lc_send.at[k], lc_recv.at[k], sibling)
+
+    def left_c_wait(k):
+        part = left.at[(layer + k) % LAYERS, pl.ds((1 - core) * half, half)]
+        remote(part, part, lc_send.at[k], lc_recv.at[k], sibling).wait_recv()
+
+    for k in (1, 3, 2):
+        left_x(k).start()
+
+    @pl.when(col != 1)
+    def _():
+        left_c(0).start()
+
+    @pl.when(jnp.logical_not(head))
+    def _():
+        def action(h, s):
+            top_wait(h, s)
+
+            @pl.when(onward)
+            def _():
+                top_copy(h, s, 0).start()
+
+            @pl.when(backward)
+            def _():
+                top_copy(h, s, 1).start()
+
+        for_top(action)
+
+    for k in (1, 3, 2):
+        left_x_wait(k)
+        left_c(LAYERS - k).start()
+
+    top_both = jnp.concatenate([top[0], top[1]], axis=1)
+    top_hi, top_lo = split(top_both)
+    up[...] = dot(inv_lp[...], top_hi) + dot(inv_lp[...], top_lo)
+    hi, lo = split(up[...])
+    up_hi[...] = hi
+    up_lo[...] = lo
+
+    @pl.when(jnp.logical_not(edge))
+    def _():
+        left_c_wait(0)
+
+    for k in range(1, LAYERS):
+        left_c_wait(k)
+
+    def send_part(r, h, d):
+        return remote(
+            red.at[h, pl.ds(pl.multiple_of(r * 256, 256), 256)],
+            out_ref.at[pl.ds(pl.multiple_of(r * 256, 256), 256), pl.ds(column(layer, h), BLOCK)],
+            ag_send.at[d, h, r], ag_recv.at[d, h, r], (to_nxt if d == 0 else to_prv),
+        )
+
+    def wait_part(r, h, d):
+        send_part(r, h, d).wait_recv()
+
+    def forward_part(r, d):
+        q = prv if d == 0 else nxt
+        part = out_ref.at[pl.ds(pl.multiple_of(r * 256, 256), 256), pl.ds(column(q, d), BLOCK)]
+        return remote(part, part, fw_send.at[d, r], fw_recv.at[d, r], (to_nxt if d == 0 else to_prv))
+
+    def compute(r, carry):
+        at = pl.ds(pl.multiple_of(r * 256, 256), 256)
+        quarter = left[r]
+        rows = jnp.concatenate([quarter[256 * j : 256 * (j + 1)] for j in range(4)], axis=1)
+        rows_hi, rows_lo = split(rows)
+        lower = dot(rows_hi, inv_u[...]) + dot(rows_lo, inv_u[...])
+        low[at] = lower
+        l_hi, l_lo = split(lower)
+        u_hi, u_lo = up_hi[...], up_lo[...]
+        change = dot(l_hi, u_hi) + (dot(l_lo, u_hi) + dot(l_hi, u_lo))
+        in_head = jnp.logical_and(head, r < 2)
+        upper = up[pl.ds(pl.multiple_of((r % 2) * 256, 256), 256)]
+        for h in range(2):
+            cut = slice(h * BLOCK, (h + 1) * BLOCK)
+            red[h, at] = jnp.where(in_head, upper[:, cut], red[h, at] - change[:, cut])
+
+        @pl.when(jnp.logical_not(edge))
+        def _():
+            send_part(r, 0, 0).start()
+            send_part(r, 0, 1).start()
+
+        send_part(r, 1, 1).start()
+        send_part(r, 1, 0).start()
+        return carry
+
+    lax.fori_loop(0, LAYERS, compute, 0)
+
+    def own_part(h):
+        return pltpu.make_async_copy(red.at[h], out_ref.at[:, pl.ds(column(layer, h), BLOCK)], out_sem.at[h])
+
+    own_part(1).start()
+
+    @pl.when(jnp.logical_not(edge))
+    def _():
+        own_part(0).start()
+
+    lower_copy = pltpu.make_async_copy(low, out_ref.at[:, pl.ds(0, half)], out_sem.at[2])
+
+    @pl.when(edge)
+    def _():
+        @pl.when(head)
+        def _():
+            quarters = []
+            for q in range(2):
+                quarters.append(jnp.concatenate([left[q, 256 * j : 256 * (j + 1)] for j in range(4)], axis=1))
+            rows = jnp.concatenate(quarters, axis=0)
+            first, rest = split(rows)
+            second, third = split(rows - first.astype(F32))
+            low[:half] = dot(perm[...], first) + dot(perm[...], second) + dot(perm[...], third)
+
+        lower_copy.start()
+
+    def pass_on(r, carry):
+        @pl.when(jnp.logical_not(edge))
+        def _():
+            wait_part(r, 0, 0)
+            forward_part(r, 0).start()
+
+        wait_part(r, 1, 1)
+        forward_part(r, 1).start()
+        return carry
+
+    lax.fori_loop(0, LAYERS, pass_on, 0)
+
+    def finish(r, carry):
+        @pl.when(jnp.logical_not(edge))
+        def _():
+            wait_part(r, 0, 1)
+            forward_wait(r, 0)
+            send_part(r, 0, 0).wait_send()
+            send_part(r, 0, 1).wait_send()
+            forward_part(r, 0).wait_send()
+
+        wait_part(r, 1, 0)
+        forward_wait(r, 1)
+        send_part(r, 1, 0).wait_send()
+        send_part(r, 1, 1).wait_send()
+        forward_part(r, 1).wait_send()
+        return carry
+
+    def forward_wait(r, d):
+        forward_part(r, d).wait_recv()
+
+    lax.fori_loop(0, LAYERS, finish, 0)
+
+    for op in relay_out + plain_out + comb_out:
+        op.wait_send()
+
+    def sent(h, s):
+        @pl.when(jnp.logical_or(head, onward))
+        def _():
+            top_copy(h, s, 0).wait_send()
+
+        @pl.when(jnp.logical_or(head, backward))
+        def _():
+            top_copy(h, s, 1).wait_send()
+
+    for_top(sent)
+
+    @pl.when(edge)
+    def _():
+        for k in range(1, GRID):
+            left_y(k).wait_send()
+
+    for k in range(1, LAYERS):
+        left_x(k).wait_send()
+        left_c(k).wait_send()
+
+    @pl.when(col != 1)
+    def _():
+        left_c(0).wait_send()
+
+    own_part(1).wait()
+
+    @pl.when(jnp.logical_not(edge))
+    def _():
+        own_part(0).wait()
+
+    @pl.when(edge)
+    def _():
+        lower_copy.wait()
+
+
+def panel(dense, separator, inverses, pivots):
+    rows, cols = separator.shape
+    half = 4 * BLOCK
+    vmem = pl.BlockSpec(memory_space=pltpu.VMEM)
+    hbm = pl.BlockSpec(memory_space=pl.ANY)
+    dma = pltpu.SemaphoreType.DMA
+    strip = (2, rows, BLOCK)
+    bf16 = jnp.bfloat16
+    return pl.pallas_call(
+        panel_kernel,
+        out_shape=jax.ShapeDtypeStruct((rows, cols), F32),
+        in_specs=[vmem, hbm, vmem, vmem],
+        out_specs=hbm,
+        scratch_shapes=[
+            pltpu.VMEM(strip, F32),
+            pltpu.VMEM(strip, F32),
+            pltpu.VMEM(strip, F32),
+            pltpu.VMEM(strip, F32),
+            pltpu.VMEM(strip, F32),
+            pltpu.VMEM((2, half, BLOCK), F32),
+            pltpu.VMEM((LAYERS, rows, BLOCK), F32),
+            pltpu.VMEM((rows, half), F32),
+            pltpu.VMEM((half, 256), bf16),
+            pltpu.VMEM((half, 256), bf16),
+            pltpu.VMEM((half, 256), F32),
+            pltpu.VMEM((half, half), bf16),
+            pltpu.VMEM((half, half), bf16),
+            pltpu.VMEM((half, half), bf16),
+            dma((6,)),
+            dma((6,)),
+            dma((6,)),
+            dma((2, 2, 2)),
+            dma((2, 2)),
+            dma((GRID,)),
+            dma,
+            dma((LAYERS,)),
+            dma((LAYERS,)),
+            dma((LAYERS,)),
+            dma((LAYERS,)),
+            dma((2, 2, LAYERS)),
+            dma((2, 2, LAYERS)),
+            dma((2, LAYERS)),
+            dma((2, LAYERS)),
+            dma((3,)),
+        ],
+        compiler_params=pltpu.CompilerParams(
+            collective_id=1, has_side_effects=True, vmem_limit_bytes=40 * 1024 * 1024
+        ),
+    )(dense, separator, inverses, pivots)
+
+
 def per_device(separator, left_factor, right_factor, owners, spots, pivot_order, panel_inverses):
-    panel_width = pivot_order.shape[0]
-    piece_rows, piece_cols = separator.shape
     dense = local_sum(left_factor, right_factor, owners, spots)
-    dense = dense.reshape(8, piece_rows, BLOCK).transpose(1, 0, 2).reshape(piece_rows, piece_cols)
-    reduced = separator - lax.psum(dense, "layer")
-    top_rows = jnp.take(reduced[:panel_width], pivot_order, axis=0)
-    left_block = reduced[:, :panel_width]
-    inverses = panel_inverses.astype(jnp.float32)
-    lower_inverse = jnp.tril(inverses, -1) + jnp.eye(panel_width, dtype=jnp.float32)
-    upper_inverse = jnp.triu(inverses)
-    upper_rows = broadcast(top_rows, "prow", 0)
-    left_columns = broadcast(left_block, "pcol", 0)
-    upper_part = jnp.dot(lower_inverse, upper_rows, precision=lax.Precision.HIGHEST)
-    lower_part = jnp.dot(left_columns, upper_inverse, precision=lax.Precision.HIGHEST)
-    trailing = reduced - jnp.dot(lower_part, upper_part, precision=lax.Precision.HIGHEST)
-    row_global = lax.axis_index("prow") * piece_rows + jnp.arange(piece_rows)
-    col_global = lax.axis_index("pcol") * piece_cols + jnp.arange(piece_cols)
-    panel_cols = col_global < panel_width
-    panel_rows = row_global < panel_width
-    widened_lower = jnp.pad(lower_part, ((0, 0), (0, piece_cols - panel_width)))
-    body_rows = jnp.where(panel_cols[None, :], widened_lower, trailing)
-    head_rows = jnp.where(panel_cols[None, :], top_rows, upper_part)
-    head_full = jnp.pad(head_rows, ((0, piece_rows - panel_width), (0, 0)))
-    return jnp.where(panel_rows[:, None], head_full, body_rows)
+    return panel(dense.reshape(8, 1024, BLOCK), separator, panel_inverses, pivot_order[:, None])
 
 
 def solution(mesh):

time: 482 us -> 282 us (0.59)
  waiting for transfers between devices: 237 us -> 0.04 us
  Pallas kernels: 113 us -> 247 us
  blocking collectives: 54.5 us -> 0 us
  matrix products: 22.5 us -> 1.55 us
  other arithmetic: 13.7 us -> 4.26 us
  local copies, waits for them, and re-layouts: 22.3 us -> 15.1 us
    psum x3 -> x0, waiting for transfers between devices: 237 us -> none  [the longest x2 137 us: broadcast(): return lax.psum(jnp.where(mine, x, jnp.zeros_like(x)), axis)]
    pallas_call x1 -> x2, Pallas kernels: 107 us -> 242 us  [the longest x1 128 us: exchange(): pl.pallas_call(exchange_kernel, out_shape=(jax.ShapeDtypeStruct((OWNERS,...]
    all_gather x1 -> x0, blocking collectives: 54.5 us -> none  [local_sum(): table = lax.all_gather(table, ('layer', 'prow', 'pcol'), axis=0, tiled=True)]
    dot_general x3 -> x0, matrix products: 20.9 us -> none  [the longest x1 8.73 us: per_device(): jnp.dot(lower_part, upper_part, precision=lax.Precision.HIGHEST)]
    unnamed x19 -> x13, local copies, waits for them, and re-layouts: 11.8 us -> 10.9 us
  transfers between devices with their start and end apart: 4 -> 1, of which waited for: 3 -> 0; matrix products, arithmetic and copies ran while one was open for 3% -> 2% of each run, Pallas kernels for 22% -> 45%
where the time goes in v2:
time: 282 us
  Pallas kernels  247 us (88%)
  local copies, waits for them, and re-layouts  15.1 us (5%)
  between operations  13.7 us (5%)
  other arithmetic  4.26 us (2%)
    pallas_call x1, Pallas kernels, exchange(): pl.pallas_call(exchange_kernel, out_shape=(jax.ShapeDtypeStruct((OWNERS,...  128 us
    pallas_call x1, Pallas kernels, panel(): pl.pallas_call(panel_kernel, out_shape=jax.ShapeDtypeStruct((rows, cols),...  114 us
    unnamed x13, local copies, waits for them, and re-layouts  10.9 us
  transfers between devices with their start and end apart: 1, of which 0 were waited for; matrix products, arithmetic and copies ran while one was open for 2% of the time, Pallas kernels for 45%

profile of v2, /device:TPU:144, one launch (start us, length us, event | category | flops | bytes accessed | tf_op | source)
XLA Modules:
  0.0 282.1 jit_solution(11479899065939682808)
XLA Ops:
  6.5 0.0 copy-start.7
  6.5 0.0 all-gather.7.cloned.1.call-start
  6.5 0.9 convert_reduce_fusion.1
  7.5 0.1 convert_reduce_fusion
  7.6 0.7 multiply_add_fusion
  8.3 0.1 select_reduce_fusion.2
  8.5 1.5 fusion.8
  10.1 0.0 all-gather.7.cloned.1.call-update
  10.1 0.6 convert_reduce_fusion.2
  10.7 0.1 fusion.18
  10.8 0.8 fusion.16
  11.6 0.8 select_reduce_fusion
  12.4 0.6 broadcast_in_dim.90
  13.1 0.1 pad_add_fusion
  13.2 128.0 %shard_map.73 = (f32[64,128,128]{2,1,0:T(8,128)S(1)}, s32[64,8,128]{2,1,0:T(8,128)S(1)}, s32[8,128]{1,0:T(8,128)S(1)}) custom-call(s32[64]{0:T(128)S(1)} %get-tuple-element.215.index_ref, s32[8,128]{1,0:T(8,128)S(1)} %broadcast_in_dim.91.table_ref, bf16[64,128,128]{2,1,0:T(8,128)(2,1)} %left_ref.1, bf16[64,128,128]{2,1,0:T(8,128)(2,1)} %right_ref.1), custom_call_target="tpu_custom_call" | custom-call | flops 268435456 | bytes 16777216 | tf_op jit(solution)/shard_map/pallas_call | solution.py:124
  141.2 0.0 copy-start.4
  141.2 2.0 copy-done.4
  143.2 0.1 copy.11
  143.3 0.6 slice.13
  144.0 0.0 copy-done.7
  144.0 0.1 copy.12.pivot_ref
  144.1 1.3 dynamic-slice_reduce_fusion
  145.4 1.3 slice_reduce_fusion
  146.8 0.0 all-gather.7.cloned.1.call-done
  146.8 0.0 copy-start.3
  146.8 2.2 copy-done.3
  149.0 0.0 copy-start.5
  149.0 2.2 copy-done.5
  151.2 5.2 %shard_map.74 = f32[64,128,128]{2,1,0:T(8,128)} custom-call(s32[64]{0:T(128)S(1)} %get-tuple-element.237.spot_ref, s32[64]{0:T(128)S(1)} %get-tuple-element.236.extra_ref, f32[64,128,128]{2,1,0:T(8,128)S(1)} %copy-done.5, f32[64,128,128]{2,1,0:T(8,128)S(1)} %bitcast.38), custom_call_target="tpu_custom_call" | custom-call | tf_op jit(solution)/shard_map/pallas_call | solution.py:189
  156.4 0.0 copy-start.6
  156.4 0.7 while.13
  157.1 0.3 copy-done.6
  157.4 0.0 copy-start.2
  157.4 2.2 copy-done.2
  159.6 113.6 %shard_map.75 = f32[1024,1024]{1,0:T(8,128)S(1)} custom-call(f32[8,1024,128]{2,1,0:T(8,128)} %bitcast.39, f32[1024,1024]{1,0:T(8,128)S(1)} %copy-done.2, bf16[512,512]{1,0:T(8,128)(2,1)S(1)} %copy-done.6, s32[512,1]{1,0:T(8,128)S(1)} %copy.12.pivot_ref), custom_call_target="tpu_custom_call" | custom-call | tf_op jit(solution)/shard_map/pallas_call | solution.py:659
  273.2 2.0 copy.22
  (6 shorter events, 0.1 us)
Async XLA Ops:
  6.5 137.4 %copy-start.7 = (s32[512]{0:T(512)S(1)}, s32[512]{0:T(512)}, u32[]{:S(2)}) copy-start(s32[512]{0:T(512)} %param.14) | copy-start | bytes 6148
  6.5 140.3 %all-gather.7.cloned.1.call-start = ((), (), s32[]{:S(2)}) async-start(), calls=%async_computation | async-start | bytes 4259840 | tf_op jit(solution)/shard_map/all_gather | solution.py:265
  141.2 2.0 copy-start.4
  146.8 2.2 copy-start.3
  149.0 2.2 copy-start.5
  156.4 1.0 copy-start.6
  157.4 2.2 copy-start.2
Sparse Core Ops, SparseCore 0:
  10.2 110.9 all-gather.6

commit v3 on v0

--- a/solution.py
+++ b/solution.py
@@ -1,7 +1,21 @@
+import functools
+
 import jax
 import jax.numpy as jnp
 from jax import lax
+from jax.experimental import pallas as pl
+from jax.experimental.pallas import tpu as pltpu
 from jax.sharding import PartitionSpec as P
+
+MESH = pl.DeviceIdType.MESH
+GRID = 8
+LAYERS = 4
+OWNERS = GRID * GRID
+BLOCK = 128
+SLICES = 4
+THIN = BLOCK // SLICES
+F32 = jnp.float32
+I32 = jnp.int32
 
 
 def broadcast(x, axis, root):
@@ -9,7 +23,7 @@
     return lax.psum(jnp.where(mine, x, jnp.zeros_like(x)), axis)
 
 
-def per_device(separator, left_factor, right_factor, owners, spots, pivot_order, panel_inverses):
+def general(separator, left_factor, right_factor, owners, spots, pivot_order, panel_inverses):
     panel_width = pivot_order.shape[0]
     update_count = left_factor.shape[0]
     block_size = left_factor.shape[1]
@@ -71,6 +85,709 @@
     return jnp.where(panel_rows[:, None], head_full, body_rows)
 
 
+def split(x):
+    high = x.astype(jnp.bfloat16)
+    return high, (x - high.astype(F32)).astype(jnp.bfloat16)
+
+
+def dot(a, b):
+    return jnp.dot(a, b, preferred_element_type=F32)
+
+
+def turned(row):
+    return jnp.broadcast_to(row, (BLOCK, BLOCK)).T
+
+
+def fused_kernel(
+    named_ref, left_ref, right_ref, sep_ref, inv_ref, pivot_ref, out_ref, peak_ref,
+    main_0, main_1, main_2, main_3, extras, out_buf, table, table_buf, peak_buf, index_buf, index_mem, sorted_buf, sorted_mem, running, dense,
+    sep_buf, relay, comb, plain, red, top, left, low, up_hi, up_lo, up, perm, inv_lp, inv_u,
+    a_send, a_recv, t_send, t_recv, p_send, p_recv, z_send, z_recv, oy_send, oy_recv, oc_send, oc_recv, mem_sem,
+    sep_sem, rs_send, rs_recv, top_send, top_recv, ly_send, ly_recv, lx_send, lx_recv, lc_send, lc_recv,
+    ag_send, ag_recv, fw_send, fw_recv, out_sem,
+):
+    layer, row, col = lax.axis_index("layer"), lax.axis_index("prow"), lax.axis_index("pcol")
+    me = row * GRID + col
+    core = col % 2
+    nxt, prv, opp = (layer + 1) % LAYERS, (layer + 3) % LAYERS, (layer + 2) % LAYERS
+    edge = col == 0
+    head = row == 0
+    half = 4 * BLOCK
+    mains = (main_0, main_1, main_2, main_3)
+
+    def remote(src, dst, send, recv, device):
+        return pltpu.make_async_remote_copy(
+            src_ref=src, dst_ref=dst, send_sem=send, recv_sem=recv, device_id=device, device_id_type=MESH
+        )
+
+    to_nxt, to_prv, to_opp = (nxt, row, col), (prv, row, col), (opp, row, col)
+    up_row, down_row = (row + 1) % GRID, (row + GRID - 1) % GRID
+    sibling = (layer, row, col + 1 - 2 * core)
+
+    def place(k):
+        return (row + k % GRID) % GRID, (col + k // GRID) % GRID
+
+    barrier = pltpu.get_barrier_semaphore()
+
+    def greet(k, carry):
+        r, c = place(k)
+        pl.semaphore_signal(barrier, inc=1, device_id=(layer, r, c), device_id_type=MESH)
+        return carry
+
+    lax.fori_loop(1, OWNERS, greet, 0)
+    for device in (to_nxt, to_prv, to_opp):
+        pl.semaphore_signal(barrier, inc=1, device_id=device, device_id_type=MESH)
+
+    def sep_first():
+        return pltpu.make_async_copy(
+            sep_ref.at[:, pl.ds(pl.multiple_of(layer * 2 * BLOCK, BLOCK), BLOCK)], sep_buf.at[0], sep_sem.at[0]
+        )
+
+    def sep_edge(j):
+        return pltpu.make_async_copy(
+            sep_ref.at[pl.ds(pl.multiple_of(layer * 256, 256), 256), pl.ds(j * BLOCK, BLOCK)],
+            sep_buf.at[0, pl.ds(j * 256, 256)],
+            sep_sem.at[2 + j],
+        )
+
+    def column(q, h):
+        normal = 2 * q + h
+        return pl.multiple_of(jnp.where(edge, 4 + q, normal) * BLOCK, BLOCK)
+
+    sep_second = pltpu.make_async_copy(
+        sep_ref.at[:, pl.ds(column(layer, 1), BLOCK)], sep_buf.at[1], sep_sem.at[1]
+    )
+    sep_second.start()
+
+    @pl.when(jnp.logical_not(edge))
+    def _():
+        sep_first().start()
+
+    @pl.when(edge)
+    def _():
+        for j in range(4):
+            sep_edge(j).start()
+
+    lane = lax.broadcasted_iota(I32, (OWNERS, BLOCK), 1)
+    line = lax.broadcasted_iota(I32, (OWNERS, BLOCK), 0)
+    named_row = jnp.broadcast_to(named_ref[...], (BLOCK, BLOCK))
+    named_col = named_row.T
+    owner_row, owner_col, spot_col = named_row[:OWNERS], named_col[:OWNERS], named_col[OWNERS:]
+
+    def down(x):
+        return jnp.sum(x, axis=0, keepdims=True)
+
+    rank = jnp.sum(jnp.where((owner_row == owner_col) & (lane < line), 1, 0), axis=1, keepdims=True)
+    rank = jnp.broadcast_to(rank, (OWNERS, BLOCK))
+    hit = (owner_col == lane) & (rank == 0)
+    index_row = down(jnp.where(hit, line, 0))
+    spot_row = down(jnp.where(hit, spot_col, 0))
+    hits = down(jnp.where(hit, 1, 0))
+    second = rank == 1
+    count_row = down(jnp.where(second, 1, 0))
+    chosen = jnp.min(jnp.where(second, line, OWNERS), axis=0, keepdims=True)
+    pick = line == chosen
+    code_row = down(jnp.where(pick, owner_col * 64 + spot_col, 0))
+    chosen_row = down(jnp.where(pick, line, 0))
+    lane_row = lax.broadcasted_iota(I32, (1, BLOCK), 1)
+    index_row = jnp.where(lane_row < OWNERS, index_row, chosen_row)
+    spot_row = jnp.where(hits > 0, spot_row, 64)
+    code_row = jnp.where(count_row > 0, code_row, -1)
+    table_row = jnp.where(lane_row < OWNERS, spot_row, jnp.where(lane_row == OWNERS, code_row, count_row))
+    table[...] = jnp.broadcast_to(table_row, (8, BLOCK))
+    index_buf[...] = jnp.broadcast_to(index_row, (8, BLOCK))
+    to_mem = pltpu.make_async_copy(index_buf, index_mem, mem_sem.at[0])
+    to_mem.start()
+    to_mem.wait()
+
+    def multiply(u):
+        return jnp.dot(left_ref[u], right_ref[u], preferred_element_type=F32)
+
+    def product(k):
+        r, c = place(k)
+        out_buf[k] = multiply(index_mem[0, r * GRID + c])
+
+    def slice_copy(k, s):
+        r, c = place(k)
+        rows = pl.ds(s * THIN, THIN)
+        return remote(
+            out_buf.at[k, rows], mains[s].at[row, col], a_send.at[s, k], a_recv.at[s, k], (layer, r, c)
+        )
+
+    def table_copy(k):
+        r, c = place(k)
+        return remote(table, table_buf.at[me], t_send.at[k], t_recv.at[k], (layer, r, c))
+
+    def peak_copy(k):
+        return remote(
+            peak_buf.at[0], peak_buf.at[k], p_send.at[k], p_recv.at[k], ((layer + k) % LAYERS, row, col)
+        )
+
+    def ring_copy(d, h):
+        source = (row + GRID - h + 1) % GRID if d == 0 else (row + h - 1) % GRID
+        part = extras.at[source, col]
+        return remote(part, part, z_send.at[d, h], z_recv.at[d, h], (layer, (up_row if d == 0 else down_row), col))
+
+    def ring_start(h):
+        ring_copy(0, h).start()
+        if h <= 3:
+            ring_copy(1, h).start()
+
+    def ring_wait(h):
+        ring_copy(0, h).wait_recv()
+        if h <= 3:
+            ring_copy(1, h).wait_recv()
+
+    def across_copy(k):
+        part = extras.at[:, col]
+        return remote(part, part, oy_send.at[k], oy_recv.at[k], (layer, row, (col + 2 * k) % GRID))
+
+    def core_copy(k):
+        part = extras.at[:, (col + GRID - 2 * k) % GRID]
+        return remote(part, part, oc_send.at[k], oc_recv.at[k], sibling)
+
+    extras[row, col] = multiply(index_mem[0, OWNERS])
+    product(1)
+    product(2)
+    pl.semaphore_wait(barrier, OWNERS - 1 + LAYERS - 1)
+    ring_start(1)
+
+    def first_slice(k, carry):
+        slice_copy(k, 0).start()
+        table_copy(k).start()
+        product(k + 2)
+        return carry
+
+    def send_slice(s):
+        def send(k, carry):
+            slice_copy(k, s).start()
+            return carry
+
+        lax.fori_loop(1, OWNERS, send, 0)
+
+    lax.fori_loop(1, 9, first_slice, 0)
+    for h in range(1, 4):
+        ring_wait(h)
+        ring_start(h + 1)
+        lax.fori_loop(1 + 8 * h, 9 + 8 * h, first_slice, 0)
+    ring_wait(4)
+    for k in (1, 3, 2):
+        across_copy(k).start()
+    core_copy(0).start()
+    lax.fori_loop(33, OWNERS - 2, first_slice, 0)
+    for k in (OWNERS - 2, OWNERS - 1):
+        slice_copy(k, 0).start()
+        table_copy(k).start()
+    own = multiply(index_mem[0, me])
+    for s in range(SLICES):
+        mains[s][row, col] = own[s * THIN : (s + 1) * THIN]
+    send_slice(1)
+
+    inv = inv_ref[...]
+    rows_at = lax.broadcasted_iota(jnp.int32, (half, half), 0)
+    cols_at = lax.broadcasted_iota(jnp.int32, (half, half), 1)
+    inv_f = inv.astype(F32)
+    lower_inverse = jnp.where(rows_at > cols_at, inv_f, jnp.where(rows_at == cols_at, 1.0, 0.0))
+    inv_u[...] = jnp.where(rows_at <= cols_at, inv_f, 0.0).astype(jnp.bfloat16)
+    perm[...] = jnp.where(pivot_ref[...] == cols_at, 1.0, 0.0).astype(jnp.bfloat16)
+    inv_lp[...] = dot(lower_inverse.astype(jnp.bfloat16), perm[...]).astype(jnp.bfloat16)
+
+    table_buf[me] = table[...]
+
+    def table_wait(k, carry):
+        table_copy(k).wait()
+        return carry
+
+    lax.fori_loop(1, OWNERS, table_wait, 0)
+    peak_buf[0] = jnp.max(table_buf[...], axis=0)
+    for k in range(1, LAYERS):
+        peak_copy(k).start()
+
+    tables = table_buf[:, 0, :]
+    mine = jnp.sum(jnp.where(lane == me, tables, 0), axis=1, keepdims=True)
+    code = jnp.sum(jnp.where(lane == OWNERS, tables, 0), axis=1, keepdims=True)
+    extra = jnp.where((code >= 0) & ((code >> 6) == me), code & 63, 64)
+    spot = jnp.concatenate([mine, extra], axis=0)
+    i, j = spot >> 3, spot & 7
+    inside = jnp.where(j < 4, (i >> 1) * 16 + j * 2 + (i & 1), (2 * (j - 4) + 1) * 8 + i)
+    slot = jnp.where(spot < 64, jnp.where(edge, inside, j * 8 + i), 64)
+    slot_col = jnp.broadcast_to(slot, (BLOCK, BLOCK))
+    slot_row = slot_col.T
+    line2 = lax.broadcasted_iota(I32, (BLOCK, BLOCK), 0)
+    lane2 = lax.broadcasted_iota(I32, (BLOCK, BLOCK), 1)
+    ahead = (slot_row < slot_col) | ((slot_row == slot_col) & (lane2 < line2))
+    rank2 = jnp.broadcast_to(jnp.sum(jnp.where(ahead, 1, 0), axis=1, keepdims=True), (BLOCK, BLOCK))
+    order_row = down(jnp.where(rank2 == lane2, line2, 0))
+    slots_row = down(jnp.where(rank2 == lane2, slot_col, 0))
+    before_row = down(jnp.where(rank2 == lane2 - 1, slot_col, 0))
+    same_row = jnp.where((slots_row == before_row) & (lane_row > 0), 1, 0)
+    last_row = down(jnp.where(slot_col <= lane2, 1, 0)) - 1
+    filled_row = jnp.where(down(jnp.where(slot_col == lane2, 1, 0)) > 0, 1, 0)
+    last_row = jnp.maximum(last_row, 0)
+    sorted_buf[0:1] = order_row
+    sorted_buf[1:2] = same_row
+    sorted_buf[2:3] = last_row
+    sorted_buf[3:4] = filled_row
+    sorted_buf[4:8] = jnp.zeros((4, BLOCK), I32)
+    to_sorted = pltpu.make_async_copy(sorted_buf, sorted_mem, mem_sem.at[1])
+    to_sorted.start()
+
+    for k in (1, 3, 2):
+        across_copy(k).wait_recv()
+        core_copy(k).start()
+    to_sorted.wait()
+    for k in range(LAYERS):
+        core_copy(k).wait_recv()
+
+    def add_up(s):
+        rows = pl.ds(s * THIN, THIN)
+
+        def run(k, total):
+            e = sorted_mem[0, k]
+            near, far = jnp.minimum(e, OWNERS - 1), jnp.maximum(e - OWNERS, 0)
+            value = jnp.where(
+                e < OWNERS, mains[s][near >> 3, near & 7], extras[far >> 3, far & 7, rows, :]
+            )
+            total = value + jnp.where(sorted_mem[1, k] == 1, total, 0.0)
+            running[k] = total
+            return total
+
+        lax.fori_loop(0, 2 * OWNERS, run, jnp.zeros((THIN, BLOCK), F32), unroll=8)
+
+        def settle(k, carry):
+            value = running[sorted_mem[2, k]]
+            dense[s, k] = jnp.where(sorted_mem[3, k] == 1, value, 0.0)
+            return carry
+
+        lax.fori_loop(0, OWNERS, settle, 0, unroll=8)
+
+    def strip(s, q):
+        return dense.at[s, pl.ds(pl.multiple_of(8 * q, 8), 8)]
+
+    def relay_out(s):
+        return [
+            remote(strip(s, 2 * opp), relay.at[0, s], rs_send.at[0, s], rs_recv.at[0, s], to_nxt),
+            remote(strip(s, 2 * opp + 1), relay.at[1, s], rs_send.at[1, s], rs_recv.at[1, s], to_prv),
+        ]
+
+    def plain_out(s):
+        return [
+            remote(strip(s, 2 * prv), plain.at[0, s], rs_send.at[2, s], rs_recv.at[2, s], to_prv),
+            remote(strip(s, 2 * nxt + 1), plain.at[1, s], rs_send.at[3, s], rs_recv.at[3, s], to_nxt),
+        ]
+
+    def comb_out(s):
+        return [
+            remote(relay.at[0, s], comb.at[0, s], rs_send.at[4, s], rs_recv.at[4, s], to_nxt),
+            remote(relay.at[1, s], comb.at[1, s], rs_send.at[5, s], rs_recv.at[5, s], to_prv),
+        ]
+
+    def combine(s):
+        relays, combs = relay_out(s), comb_out(s)
+        for h, q in ((0, 2 * nxt), (1, 2 * prv + 1)):
+            relays[h].wait_recv()
+            relay[h, s] += dense[s, pl.ds(pl.multiple_of(8 * q, 8), 8)]
+            combs[h].start()
+
+    for s in range(SLICES):
+        def slice_wait(k, carry):
+            slice_copy(k, s).wait_recv()
+            return carry
+
+        lax.fori_loop(1, OWNERS, slice_wait, 0)
+        add_up(s)
+        for op in relay_out(s) + plain_out(s):
+            op.start()
+        if s + 2 < SLICES:
+            send_slice(s + 2)
+        if s >= 1:
+            combine(s - 1)
+    combine(SLICES - 1)
+
+    @pl.when(jnp.logical_not(edge))
+    def _():
+        sep_first().wait()
+
+    @pl.when(edge)
+    def _():
+        for j in range(4):
+            sep_edge(j).wait()
+
+    sep_second.wait()
+
+    def reduced(s, carry):
+        plains, combs = plain_out(s), comb_out(s)
+        for h in range(2):
+            plains[h].wait_recv()
+            combs[h].wait_recv()
+            for b in range(8):
+                at = pl.ds(pl.multiple_of(b * BLOCK + s * THIN, THIN), THIN)
+                red[h, at] = sep_buf[h, at] - (dense[s, 8 * (2 * layer + h) + b] + plain[h, s, b] + comb[h, s, b])
+        return carry
+
+    lax.fori_loop(0, SLICES, reduced, 0)
+
+    def exchange_sent():
+        def one(k, carry):
+            for s in range(SLICES):
+                slice_copy(k, s).wait_send()
+            return carry
+
+        lax.fori_loop(1, OWNERS, one, 0)
+        for k in range(1, LAYERS):
+            peak_copy(k).wait()
+            across_copy(k).wait_send()
+        for k in range(LAYERS):
+            core_copy(k).wait_send()
+        for h in range(1, 5):
+            ring_copy(0, h).wait_send()
+            if h <= 3:
+                ring_copy(1, h).wait_send()
+        peak_ref[...] = jnp.max(peak_buf[...], axis=0)
+
+    def top_copy(h, s, d):
+        part = top.at[h, pl.ds(s * 256, 256)]
+        return remote(
+            part, part, top_send.at[d, h, s], top_recv.at[h, s],
+            (layer, (up_row if d == 0 else down_row), col),
+        )
+
+    def top_wait(h, s):
+        top_copy(h, s, 0).wait_recv()
+
+    onward = jnp.logical_and(row >= 1, row <= 3)
+    backward = row >= 6
+
+    def for_top(action):
+        for h in (1, 0):
+            for s in range(2):
+                if h == 1:
+                    action(h, s)
+                else:
+                    pl.when(jnp.logical_not(edge))(functools.partial(action, h, s))
+
+    @pl.when(head)
+    def _():
+        top[0] = red[0, :half]
+        top[1] = red[1, :half]
+
+        def action(h, s):
+            top_copy(h, s, 0).start()
+            top_copy(h, s, 1).start()
+
+        for_top(action)
+
+    @pl.when(jnp.logical_and(edge, jnp.logical_not(head)))
+    def _():
+        top[0] = jnp.zeros((half, BLOCK), F32)
+
+    def left_y(k):
+        c = (col + k) % GRID
+        part = left.at[layer, pl.ds((c % 2) * half, half)]
+        return remote(part, part, ly_send.at[k], ly_recv, (layer, row, c))
+
+    @pl.when(edge)
+    def _():
+        left[layer] = red[0]
+        for k in (2, 3, 6, 7, 4, 5, 1):
+            left_y(k).start()
+
+    @pl.when(jnp.logical_not(edge))
+    def _():
+        mine = left.at[layer, pl.ds(core * half, half)]
+        remote(mine, mine, ly_send.at[0], ly_recv, (layer, row, (col + 1) % GRID)).wait_recv()
+
+    def left_x(k):
+        part = left.at[layer, pl.ds(core * half, half)]
+        return remote(part, part, lx_send.at[k], lx_recv.at[k], ((layer + k) % LAYERS, row, col))
+
+    def left_x_wait(k):
+        part = left.at[(layer + LAYERS - k) % LAYERS, pl.ds(core * half, half)]
+        remote(part, part, lx_send.at[k], lx_recv.at[k], ((layer + k) % LAYERS, row, col)).wait_recv()
+
+    sibling = (layer, row, col + 1 - 2 * core)
+
+    def left_c(k):
+        part = left.at[(layer + k) % LAYERS, pl.ds(core * half, half)]
+        return remote(part, part, lc_send.at[k], lc_recv.at[k], sibling)
+
+    def left_c_wait(k):
+        part = left.at[(layer + k) % LAYERS, pl.ds((1 - core) * half, half)]
+        remote(part, part, lc_send.at[k], lc_recv.at[k], sibling).wait_recv()
+
+    for k in (1, 3, 2):
+        left_x(k).start()
+
+    @pl.when(col != 1)
+    def _():
+        left_c(0).start()
+
+    @pl.when(jnp.logical_not(head))
+    def _():
+        def action(h, s):
+            top_wait(h, s)
+
+            @pl.when(onward)
+            def _():
+                top_copy(h, s, 0).start()
+
+            @pl.when(backward)
+            def _():
+                top_copy(h, s, 1).start()
+
+        for_top(action)
+
+    for k in (1, 3, 2):
+        left_x_wait(k)
+        left_c(LAYERS - k).start()
+
+    top_both = jnp.concatenate([top[0], top[1]], axis=1)
+    top_hi, top_lo = split(top_both)
+    up[...] = dot(inv_lp[...], top_hi) + dot(inv_lp[...], top_lo)
+    hi, lo = split(up[...])
+    up_hi[...] = hi
+    up_lo[...] = lo
+
+    @pl.when(jnp.logical_not(edge))
+    def _():
+        left_c_wait(0)
+
+    for k in range(1, LAYERS):
+        left_c_wait(k)
+
+    def send_part(r, h, d):
+        return remote(
+            red.at[h, pl.ds(pl.multiple_of(r * 256, 256), 256)],
+            out_ref.at[pl.ds(pl.multiple_of(r * 256, 256), 256), pl.ds(column(layer, h), BLOCK)],
+            ag_send.at[d, h, r], ag_recv.at[d, h, r], (to_nxt if d == 0 else to_prv),
+        )
+
+    def wait_part(r, h, d):
+        send_part(r, h, d).wait_recv()
+
+    def forward_part(r, d):
+        q = prv if d == 0 else nxt
+        part = out_ref.at[pl.ds(pl.multiple_of(r * 256, 256), 256), pl.ds(column(q, d), BLOCK)]
+        return remote(part, part, fw_send.at[d, r], fw_recv.at[d, r], (to_nxt if d == 0 else to_prv))
+
+    def compute(r, carry):
+        at = pl.ds(pl.multiple_of(r * 256, 256), 256)
+        quarter = left[r]
+        rows = jnp.concatenate([quarter[256 * j : 256 * (j + 1)] for j in range(4)], axis=1)
+        rows_hi, rows_lo = split(rows)
+        lower = dot(rows_hi, inv_u[...]) + dot(rows_lo, inv_u[...])
+        low[at] = lower
+        l_hi, l_lo = split(lower)
+        u_hi, u_lo = up_hi[...], up_lo[...]
+        change = dot(l_hi, u_hi) + (dot(l_lo, u_hi) + dot(l_hi, u_lo))
+        in_head = jnp.logical_and(head, r < 2)
+        upper = up[pl.ds(pl.multiple_of((r % 2) * 256, 256), 256)]
+        for h in range(2):
+            cut = slice(h * BLOCK, (h + 1) * BLOCK)
+            red[h, at] = jnp.where(in_head, upper[:, cut], red[h, at] - change[:, cut])
+
+        @pl.when(jnp.logical_not(edge))
+        def _():
+            send_part(r, 0, 0).start()
+            send_part(r, 0, 1).start()
+
+        send_part(r, 1, 1).start()
+        send_part(r, 1, 0).start()
+        return carry
+
+    lax.fori_loop(0, LAYERS, compute, 0)
+
+    def own_part(h):
+        return pltpu.make_async_copy(red.at[h], out_ref.at[:, pl.ds(column(layer, h), BLOCK)], out_sem.at[h])
+
+    own_part(1).start()
+
+    @pl.when(jnp.logical_not(edge))
+    def _():
+        own_part(0).start()
+
+    lower_copy = pltpu.make_async_copy(low, out_ref.at[:, pl.ds(0, half)], out_sem.at[2])
+
+    @pl.when(edge)
+    def _():
+        @pl.when(head)
+        def _():
+            quarters = []
+            for q in range(2):
+                quarters.append(jnp.concatenate([left[q, 256 * j : 256 * (j + 1)] for j in range(4)], axis=1))
+            rows = jnp.concatenate(quarters, axis=0)
+            first, rest = split(rows)
+            second, third = split(rows - first.astype(F32))
+            low[:half] = dot(perm[...], first) + dot(perm[...], second) + dot(perm[...], third)
+
+        lower_copy.start()
+
+    def pass_on(r, carry):
+        @pl.when(jnp.logical_not(edge))
+        def _():
+            wait_part(r, 0, 0)
+            forward_part(r, 0).start()
+
+        wait_part(r, 1, 1)
+        forward_part(r, 1).start()
+        return carry
+
+    lax.fori_loop(0, LAYERS, pass_on, 0)
+
+    def finish(r, carry):
+        @pl.when(jnp.logical_not(edge))
+        def _():
+            wait_part(r, 0, 1)
+            forward_wait(r, 0)
+            send_part(r, 0, 0).wait_send()
+            send_part(r, 0, 1).wait_send()
+            forward_part(r, 0).wait_send()
+
+        wait_part(r, 1, 0)
+        forward_wait(r, 1)
+        send_part(r, 1, 0).wait_send()
+        send_part(r, 1, 1).wait_send()
+        forward_part(r, 1).wait_send()
+        return carry
+
+    def forward_wait(r, d):
+        forward_part(r, d).wait_recv()
+
+    lax.fori_loop(0, LAYERS, finish, 0)
+
+    def sum_sent(s, carry):
+        for op in relay_out(s) + plain_out(s) + comb_out(s):
+            op.wait_send()
+        return carry
+
+    lax.fori_loop(0, SLICES, sum_sent, 0)
+    exchange_sent()
+
+    def sent(h, s):
+        @pl.when(jnp.logical_or(head, onward))
+        def _():
+            top_copy(h, s, 0).wait_send()
+
+        @pl.when(jnp.logical_or(head, backward))
+        def _():
+            top_copy(h, s, 1).wait_send()
+
+    for_top(sent)
+
+    @pl.when(edge)
+    def _():
+        for k in range(1, GRID):
+            left_y(k).wait_send()
+
+    for k in range(1, LAYERS):
+        left_x(k).wait_send()
+        left_c(k).wait_send()
+
+    @pl.when(col != 1)
+    def _():
+        left_c(0).wait_send()
+
+    own_part(1).wait()
+
+    @pl.when(jnp.logical_not(edge))
+    def _():
+        own_part(0).wait()
+
+    @pl.when(edge)
+    def _():
+        lower_copy.wait()
+
+
+def fused(named, left, right, separator, inverses, pivots):
+    rows, cols = separator.shape
+    half = 4 * BLOCK
+    vmem = pl.BlockSpec(memory_space=pltpu.VMEM)
+    hbm = pl.BlockSpec(memory_space=pl.ANY)
+    dma = pltpu.SemaphoreType.DMA
+    strip = (2, rows, BLOCK)
+    thin = (2, SLICES, 8, THIN, BLOCK)
+    bf16 = jnp.bfloat16
+    return pl.pallas_call(
+        fused_kernel,
+        out_shape=(jax.ShapeDtypeStruct((rows, cols), F32), jax.ShapeDtypeStruct((8, BLOCK), I32)),
+        in_specs=[vmem, vmem, vmem, hbm, vmem, vmem],
+        out_specs=(hbm, vmem),
+        scratch_shapes=[
+            pltpu.VMEM((GRID, GRID, THIN, BLOCK), F32),
+            pltpu.VMEM((GRID, GRID, THIN, BLOCK), F32),
+            pltpu.VMEM((GRID, GRID, THIN, BLOCK), F32),
+            pltpu.VMEM((GRID, GRID, THIN, BLOCK), F32),
+            pltpu.VMEM((GRID, GRID, BLOCK, BLOCK), F32),
+            pltpu.VMEM((OWNERS, BLOCK, BLOCK), F32),
+            pltpu.VMEM((8, BLOCK), I32),
+            pltpu.VMEM((OWNERS, 8, BLOCK), I32),
+            pltpu.VMEM((LAYERS, 8, BLOCK), I32),
+            pltpu.VMEM((8, BLOCK), I32),
+            pltpu.SMEM((8, BLOCK), I32),
+            pltpu.VMEM((8, BLOCK), I32),
+            pltpu.SMEM((8, BLOCK), I32),
+            pltpu.VMEM((2 * OWNERS, THIN, BLOCK), F32),
+            pltpu.VMEM((SLICES, OWNERS, THIN, BLOCK), F32),
+            pltpu.VMEM(strip, F32),
+            pltpu.VMEM(thin, F32),
+            pltpu.VMEM(thin, F32),
+            pltpu.VMEM(thin, F32),
+            pltpu.VMEM(strip, F32),
+            pltpu.VMEM((2, half, BLOCK), F32),
+            pltpu.VMEM((LAYERS, rows, BLOCK), F32),
+            pltpu.VMEM((rows, half), F32),
+            pltpu.VMEM((half, 256), bf16),
+            pltpu.VMEM((half, 256), bf16),
+            pltpu.VMEM((half, 256), F32),
+            pltpu.VMEM((half, half), bf16),
+            pltpu.VMEM((half, half), bf16),
+            pltpu.VMEM((half, half), bf16),
+            dma((SLICES, OWNERS)),
+            dma((SLICES, OWNERS)),
+            dma((OWNERS,)),
+            dma((OWNERS,)),
+            dma((LAYERS,)),
+            dma((LAYERS,)),
+            dma((2, 5)),
+            dma((2, 5)),
+            dma((LAYERS,)),
+            dma((LAYERS,)),
+            dma((LAYERS,)),
+            dma((LAYERS,)),
+            dma((2,)),
+            dma((6,)),
+            dma((6, SLICES)),
+            dma((6, SLICES)),
+            dma((2, 2, 2)),
+            dma((2, 2)),
+            dma((GRID,)),
+            dma,
+            dma((LAYERS,)),
+            dma((LAYERS,)),
+            dma((LAYERS,)),
+            dma((LAYERS,)),
+            dma((2, 2, LAYERS)),
+            dma((2, 2, LAYERS)),
+            dma((2, LAYERS)),
+            dma((2, LAYERS)),
+            dma((3,)),
+        ],
+        compiler_params=pltpu.CompilerParams(
+            collective_id=0, has_side_effects=True, vmem_limit_bytes=56 * 1024 * 1024
+        ),
+    )(named, left, right, separator, inverses, pivots)
+
+
+def per_device(separator, left_factor, right_factor, owners, spots, pivot_order, panel_inverses):
+    named = jnp.concatenate([owners[:, 0], spots])[None, :]
+    result, peak = fused(named, left_factor, right_factor, separator, panel_inverses, pivot_order[:, None])
+    return lax.cond(
+        peak[0, BLOCK - 1] > 1,
+        lambda: general(separator, left_factor, right_factor, owners, spots, pivot_order, panel_inverses),
+        lambda: result,
+    )
+
+
 def solution(mesh):
     in_specs = (
         P("prow", "pcol"),
@@ -81,7 +798,6 @@
         P(),
         P(),
     )
-    out_specs = P("prow", "pcol")
     return jax.shard_map(
-        per_device, mesh=mesh, in_specs=in_specs, out_specs=out_specs, check_vma=False
+        per_device, mesh=mesh, in_specs=in_specs, out_specs=P("prow", "pcol"), check_vma=False
     )

time: 551 us -> 244 us (0.44)
  waiting for transfers between devices: 418 us -> 0 us
  Pallas kernels: 0 us -> 223 us
  local copies, waits for them, and re-layouts: 43.8 us -> 4.83 us
  matrix products: 38.9 us -> 0 us
  starting transfers between devices: 21.1 us -> 0 us
  other arithmetic: 11.4 us -> 1.32 us
    psum x3 -> x0, waiting for transfers between devices: 239 us -> none  [the longest x2 138 us: broadcast(): return lax.psum(jnp.where(mine, x, jnp.zeros_like(x)), axis)]
    pallas_call x0 -> x1, Pallas kernels: none -> 223 us  [fused(): pl.pallas_call(fused_kernel, out_shape=(jax.ShapeDtypeStruct((rows, cols)...]
    all_to_all x2 -> x0, waiting for transfers between devices: 179 us -> none  [the longest x1 179 us: per_device(): lax.all_to_all(outgoing, ('prow', 'pcol'), split_axis=0, concat_axis=0, t...]
    dot_general x7 -> x0, matrix products: 38.9 us -> none  [the longest x1 8.72 us: per_device(): jnp.dot(lower_part, upper_part, precision=lax.Precision.HIGHEST)]
    all_to_all x2 -> x0, starting transfers between devices: 20.8 us -> none  [the longest x1 10.5 us: per_device(): lax.all_to_all(outgoing, ('prow', 'pcol'), split_axis=0, concat_axis=0, t...]
    dot_general x2 -> x0, local copies, waits for them, and re-layouts: 16.8 us -> none  [the longest x1 9.01 us: per_device(): jnp.einsum('rp,rq->pq', placing, arrived, precision=lax.Precision.HIGHEST)]
    all_to_all x3 -> x0, local copies, waits for them, and re-layouts: 12.1 us -> none  [the longest x1 10.9 us: per_device(): lax.all_to_all(outgoing, ('prow', 'pcol'), split_axis=0, concat_axis=0, t...]
  transfers between devices with their start and end apart: 5 -> 0, of which waited for: 4 -> 0; matrix products, arithmetic and copies ran while one was open for 7% -> 0% of each run, Pallas kernels for 0% -> 0%
where the time goes in v3:
time: 244 us
  Pallas kernels  223 us (91%)
  between operations  14.1 us (6%)
  local copies, waits for them, and re-layouts  4.83 us (2%)
    pallas_call x1, Pallas kernels, fused(): pl.pallas_call(fused_kernel, out_shape=(jax.ShapeDtypeStruct((rows, cols)...  223 us

profile of v3, /device:TPU:144, one launch (start us, length us, event | category | flops | bytes accessed | tf_op | source)
XLA Modules:
  0.0 243.8 jit_solution(9421468696932141366)
XLA Ops:
  6.5 1.5 copy.20.pivot_ref
  8.1 1.3 add_bitcast_fusion.named_ref
  9.4 0.0 copy-start.4
  9.4 0.0 copy-start.5
  9.4 0.0 copy-start.6
  9.4 0.0 copy-start.7
  9.4 0.0 copy-start.8
  9.4 223.3 %shard_map.75 = (f32[1024,1024]{1,0:T(8,128)S(1)}, s32[8,128]{1,0:T(8,128)}) custom-call(s32[1,128]{1,0:T(1,128)} %add_bitcast_fusion.named_ref, bf16[64,128,128]{2,1,0:T(8,128)(2,1)} %left_ref.1, bf16[64,128,128]{2,1,0:T(8,128)(2,1)} %right_ref.1, f32[1024,1024]{1,0:T(8,128)} %sep_ref.1, bf16[512,512]{1,0:T(8,128)(2,1)} %inv_ref.1, s32[512,1]{1,0:T(8,128)} %copy.20.pivot_ref), custom_call_target="tpu_custom_call" | custom-call | tf_op jit(solution)/shard_map/pallas_call | solution.py:710
  232.8 1.3 slice.9
  234.7 0.0 copy-done.4
  234.7 0.0 copy-done.5
  234.7 0.0 copy-done.6
  234.7 0.0 copy-done.7
  234.7 0.0 copy-done.8
  234.7 0.2 conditional.1
  235.0 2.0 copy.31
Async XLA Ops:
  9.4 225.3 %copy-start.4 = (bf16[64,128,128]{2,1,0:T(8,128)(2,1)S(1)}, bf16[64,128,128]{2,1,0:T(8,128)(2,1)}, u32[]{:S(2)}) copy-start(bf16[64,128,128]{2,1,0:T(8,128)(2,1)} %left_ref.1) | copy-start | bytes 6291460
  9.4 225.3 %copy-start.5 = (bf16[512,512]{1,0:T(8,128)(2,1)S(1)}, bf16[512,512]{1,0:T(8,128)(2,1)}, u32[]{:S(2)}) copy-start(bf16[512,512]{1,0:T(8,128)(2,1)} %inv_ref.1) | copy-start | bytes 1572868
  9.4 225.3 %copy-start.6 = (s32[512]{0:T(512)S(1)}, s32[512]{0:T(512)}, u32[]{:S(2)}) copy-start(s32[512]{0:T(512)} %param.14) | copy-start | bytes 6148
  9.4 225.3 %copy-start.7 = (s32[64]{0:T(128)S(1)}, s32[64]{0:T(128)}, u32[]{:S(2)}) copy-start(s32[64]{0:T(128)} %param.13) | copy-start | bytes 772
  9.4 225.3 %copy-start.8 = (s32[64,1]{0,1:T(1,128)S(1)}, s32[64,1]{0,1:T(1,128)}, u32[]{:S(2)}) copy-start(s32[64,1]{0,1:T(1,128)} %param.12) | copy-start | bytes 772

commit v4 on v2

--- a/solution.py
+++ b/solution.py
@@ -12,23 +12,46 @@
 LAYERS = 4
 OWNERS = GRID * GRID
 BLOCK = 128
+THINS = (32, 32, 32, 32)
+STARTS = tuple(sum(THINS[:s]) for s in range(len(THINS)))
+SLICES = len(THINS)
+AHEAD = 2
+EARLY = 16
 F32 = jnp.float32
+BF16 = jnp.bfloat16
+I32 = jnp.int32
+
+
+def split(x):
+    high = x.astype(BF16)
+    return high, (x - high.astype(F32)).astype(BF16)
+
+
+def dot(a, b):
+    return jnp.dot(a, b, preferred_element_type=F32)
+
+
+def down(x):
+    return jnp.sum(x, axis=0, keepdims=True)
+
+
+def across(x):
+    return jnp.sum(x, axis=1, keepdims=True)
+
+
+def wide(x):
+    return jnp.broadcast_to(x, (x.shape[0], BLOCK))
 
 
 def exchange_kernel(
-    index_ref, table_ref, left_ref, right_ref, recv_ref, tables_ref, peak_ref,
-    out_buf, table_buf, peak_buf, send_sem, recv_sem, own_sem, table_send, table_recv, peak_send, peak_recv,
+    index_ref, table_ref, left_ref, right_ref, recv_ref, tables_ref,
+    out_buf, table_buf, send_sem, recv_sem, own_sem, table_send, table_recv,
 ):
     layer, row, col = lax.axis_index("layer"), lax.axis_index("prow"), lax.axis_index("pcol")
     me = row * GRID + col
 
     def place(k):
-        r = (row + k % GRID) % GRID
-        c = (col + k // GRID) % GRID
-        return r, c
-
-    def other(k):
-        return ((layer + k) % LAYERS, row, col)
+        return (row + k % GRID) % GRID, (col + k // GRID) % GRID
 
     barrier = pltpu.get_barrier_semaphore()
 
@@ -38,13 +61,12 @@
         return carry
 
     lax.fori_loop(1, OWNERS, greet, 0)
-    for k in range(1, LAYERS):
-        pl.semaphore_signal(barrier, inc=1, device_id=other(k), device_id_type=MESH)
 
     def product(k):
         r, c = place(k)
-        u = index_ref[r * GRID + c]
-        out_buf[k] = jnp.dot(left_ref[u], right_ref[u], preferred_element_type=F32)
+        for t in range(2):
+            u = index_ref[t * OWNERS + r * GRID + c]
+            out_buf[k, t] = jnp.dot(left_ref[u], right_ref[u], preferred_element_type=F32)
 
     def copy(k):
         r, c = place(k)
@@ -68,90 +90,57 @@
             device_id_type=MESH,
         )
 
-    def peak_copy(k):
-        return pltpu.make_async_remote_copy(
-            src_ref=peak_buf.at[0],
-            dst_ref=peak_buf.at[k],
-            send_sem=peak_send.at[k],
-            recv_sem=peak_recv.at[k],
-            device_id=other(k),
-            device_id_type=MESH,
-        )
-
-    product(0)
-    product(1)
-    pl.semaphore_wait(barrier, OWNERS - 1 + LAYERS - 1)
-
-    def send_table(k, carry):
+    pl.semaphore_wait(barrier, OWNERS - 1)
+
+    def send(k, carry):
+        product(k)
+        copy(k).start()
         table_copy(k).start()
         return carry
 
-    def send(k, carry):
-        copy(k).start()
-        product(k + 1)
-        return carry
-
-    lax.fori_loop(1, OWNERS - 1, send, 0)
-    copy(OWNERS - 1).start()
-    lax.fori_loop(1, OWNERS, send_table, 0)
+    lax.fori_loop(1, OWNERS, send, 0)
+    product(0)
     own = pltpu.make_async_copy(out_buf.at[0], recv_ref.at[me], own_sem)
     own.start()
     table_buf[me] = table_ref[...]
 
-    def finish_table(k, carry):
+    def finish(k, carry):
         table_copy(k).wait()
-        return carry
-
-    lax.fori_loop(1, OWNERS, finish_table, 0)
-    tables_ref[...] = table_buf[...]
-    peak_buf[0] = jnp.max(table_buf[...], axis=0)
-    for k in range(1, LAYERS):
-        peak_copy(k).start()
-    own.wait()
-
-    def finish(k, carry):
         copy(k).wait()
         return carry
 
     lax.fori_loop(1, OWNERS, finish, 0)
-    for k in range(1, LAYERS):
-        peak_copy(k).wait()
-    peak_ref[...] = jnp.max(peak_buf[...], axis=0)
+    own.wait()
+    tables_ref[...] = table_buf[...]
 
 
 def exchange(index, table, left, right):
     vmem = pl.BlockSpec(memory_space=pltpu.VMEM)
+    dma = pltpu.SemaphoreType.DMA
     return pl.pallas_call(
         exchange_kernel,
         out_shape=(
-            jax.ShapeDtypeStruct((OWNERS, BLOCK, BLOCK), F32),
-            jax.ShapeDtypeStruct((OWNERS, 8, BLOCK), jnp.int32),
-            jax.ShapeDtypeStruct((8, BLOCK), jnp.int32),
+            jax.ShapeDtypeStruct((OWNERS, 2, BLOCK, BLOCK), F32),
+            jax.ShapeDtypeStruct((OWNERS, 8, BLOCK), I32),
         ),
         in_specs=[pl.BlockSpec(memory_space=pltpu.SMEM), vmem, vmem, vmem],
-        out_specs=(pl.BlockSpec(memory_space=pl.ANY), vmem, vmem),
+        out_specs=(pl.BlockSpec(memory_space=pl.ANY), vmem),
         scratch_shapes=[
-            pltpu.VMEM((OWNERS, BLOCK, BLOCK), F32),
-            pltpu.VMEM((OWNERS, 8, BLOCK), jnp.int32),
-            pltpu.VMEM((LAYERS, 8, BLOCK), jnp.int32),
-            pltpu.SemaphoreType.DMA((OWNERS,)),
-            pltpu.SemaphoreType.DMA((OWNERS,)),
-            pltpu.SemaphoreType.DMA,
-            pltpu.SemaphoreType.DMA((OWNERS,)),
-            pltpu.SemaphoreType.DMA((OWNERS,)),
-            pltpu.SemaphoreType.DMA((LAYERS,)),
-            pltpu.SemaphoreType.DMA((LAYERS,)),
+            pltpu.VMEM((OWNERS, 2, BLOCK, BLOCK), F32),
+            pltpu.VMEM((OWNERS, 8, BLOCK), I32),
+            dma((OWNERS,)),
+            dma((OWNERS,)),
+            dma,
+            dma((OWNERS,)),
+            dma((OWNERS,)),
         ],
         compiler_params=pltpu.CompilerParams(
-            collective_id=0, has_side_effects=True, vmem_limit_bytes=32 * 1024 * 1024
-        ),
-        cost_estimate=pl.CostEstimate(
-            flops=2 * OWNERS * BLOCK**3, bytes_accessed=16 * 1024 * 1024, transcendentals=0
+            collective_id=1, has_side_effects=True, vmem_limit_bytes=32 * 1024 * 1024
         ),
     )(index, table, left, right)
 
 
-def scatter_kernel(per_step, spot_ref, extra_ref, recv_ref, extra_hbm, out_ref, extra_buf, extra_sem):
+def scatter_kernel(slot_ref, recv_ref, out_ref):
     step = pl.program_id(0)
 
     @pl.when(step == 0)
@@ -159,136 +148,29 @@
         out_ref[...] = jnp.zeros_like(out_ref)
 
     def add(k, carry):
-        spot = spot_ref[step * per_step + k]
-
-        @pl.when(spot < 64)
-        def _():
-            out_ref[spot] += recv_ref[k]
+        slot = slot_ref[step * 8 + k]
+
+        @pl.when(slot < 64)
+        def _():
+            out_ref[slot] += recv_ref[k]
 
         return carry
 
-    lax.fori_loop(0, per_step, add, 0)
-
-    def add_extra(k, carry):
-        spot = extra_ref[step * per_step + k]
-
-        @pl.when(spot < 64)
-        def _():
-            fetch = pltpu.make_async_copy(extra_hbm.at[step * per_step + k], extra_buf, extra_sem)
-            fetch.start()
-            fetch.wait()
-            out_ref[spot] += extra_buf[...]
-
-        return carry
-
-    lax.fori_loop(0, per_step, add_extra, 0)
-
-
-def scatter(spots, extra_spots, recv, extra):
-    per_step = 8
+    lax.fori_loop(0, 8, add, 0)
+
+
+def scatter(slots, recv):
     return pl.pallas_call(
-        functools.partial(scatter_kernel, per_step),
+        scatter_kernel,
         out_shape=jax.ShapeDtypeStruct((64, BLOCK, BLOCK), F32),
-        grid=(OWNERS // per_step,),
+        grid=(2 * OWNERS // 8,),
         in_specs=[
             pl.BlockSpec(memory_space=pltpu.SMEM),
-            pl.BlockSpec(memory_space=pltpu.SMEM),
-            pl.BlockSpec((per_step, BLOCK, BLOCK), lambda i: (i, 0, 0)),
-            pl.BlockSpec(memory_space=pl.ANY),
+            pl.BlockSpec((8, BLOCK, BLOCK), lambda i: (i, 0, 0)),
         ],
         out_specs=pl.BlockSpec((64, BLOCK, BLOCK), lambda i: (0, 0, 0)),
-        scratch_shapes=[pltpu.VMEM((BLOCK, BLOCK), F32), pltpu.SemaphoreType.DMA],
         compiler_params=pltpu.CompilerParams(vmem_limit_bytes=24 * 1024 * 1024),
-    )(spots, extra_spots, recv, extra)
-
-
-def scatter_extra_kernel(extra_ref, dense_ref, extra_ref_data, out_ref):
-    out_ref[...] = dense_ref[...]
-
-    def add(k, carry):
-        spot = extra_ref[k]
-
-        @pl.when(spot < 64)
-        def _():
-            out_ref[spot] += extra_ref_data[k]
-
-        return carry
-
-    lax.fori_loop(0, OWNERS, add, 0)
-
-
-def scatter_extra(extra_spots, dense, extra):
-    return pl.pallas_call(
-        scatter_extra_kernel,
-        out_shape=jax.ShapeDtypeStruct((64, BLOCK, BLOCK), F32),
-        in_specs=[
-            pl.BlockSpec(memory_space=pltpu.SMEM),
-            pl.BlockSpec(memory_space=pltpu.VMEM),
-            pl.BlockSpec(memory_space=pltpu.VMEM),
-        ],
-        out_specs=pl.BlockSpec(memory_space=pltpu.VMEM),
-        compiler_params=pltpu.CompilerParams(vmem_limit_bytes=24 * 1024 * 1024),
-    )(extra_spots, dense, extra)
-
-
-def local_sum(left, right, owners, spots):
-    update_count = left.shape[0]
-    most = update_count // 2
-    destination = owners[:, 0]
-    counter = jnp.arange(update_count)
-    same = destination[:, None] == destination[None, :]
-    rank = jnp.sum(same & (counter[None, :] < counter[:, None]), axis=1)
-    named = (destination[None, :] == jnp.arange(OWNERS)[:, None]) & (rank == 0)[None, :]
-    index = jnp.sum(jnp.where(named, counter[None, :], 0), axis=1)
-    first_spot = jnp.sum(jnp.where(named, spots[None, :], 0), axis=1)
-    first_spot = jnp.where(jnp.any(named, axis=1), first_spot, 64)
-    second = rank == 1
-    order = jnp.sum(second[None, :] & (counter[None, :] < counter[:, None]), axis=1)
-    picked = second[None, :] & (order[None, :] == jnp.arange(most)[:, None])
-    extra_index = jnp.sum(jnp.where(picked, counter[None, :], 0), axis=1)
-    extra_code = jnp.sum(jnp.where(picked, destination[None, :] * 64 + spots[None, :], 0), axis=1)
-    extra_code = jnp.where(jnp.any(picked, axis=1), extra_code, -1)
-    count = jnp.sum(second).astype(jnp.int32)
-    table = jnp.concatenate([first_spot, extra_code, jnp.full((32,), count)]).astype(jnp.int32)
-    table = jnp.broadcast_to(table[None, :], (8, 128))
-    col = lax.axis_index("pcol")
-    me = lax.axis_index("prow") * GRID + col
-
-    def slot_of(spot):
-        i, j = spot // 8, spot % 8
-        inside = jnp.where(j < 4, (i // 2) * 16 + j * 2 + i % 2, (2 * (j - 4) + 1) * 8 + i)
-        return jnp.where(spot < 64, jnp.where(col == 0, inside, j * 8 + i), 64)
-
-    def extra_round(k):
-        u = extra_index[k]
-        block = jnp.dot(left[u], right[u], preferred_element_type=F32)
-        blocks = lax.all_gather(block[None], ("prow", "pcol"), axis=0, tiled=True)
-        code = lax.dynamic_index_in_dim(layer_table, OWNERS + k, 1, keepdims=False)
-        extra_spots = jnp.where((code >= 0) & (code // 64 == me), code % 64, 64)
-        return slot_of(extra_spots), blocks
-
-    recv, tables, peak = exchange(index, table, left, right)
-    layer_table = tables[:, 0, :]
-    rounds = peak[0, 96]
-    my_spots = slot_of(lax.dynamic_index_in_dim(layer_table, me, 1, keepdims=False))
-    extra_spots, blocks = extra_round(0)
-    dense = scatter(my_spots, extra_spots, recv, blocks)
-
-    def body(carry):
-        k, dense = carry
-        extra_spots, blocks = extra_round(k)
-        return k + 1, scatter_extra(extra_spots, dense, blocks)
-
-    return lax.while_loop(lambda carry: carry[0] < rounds, body, (jnp.int32(1), dense))[1]
-
-
-def split(x):
-    high = x.astype(jnp.bfloat16)
-    return high, (x - high.astype(F32)).astype(jnp.bfloat16)
-
-
-def dot(a, b):
-    return jnp.dot(a, b, preferred_element_type=F32)
+    )(slots, recv)
 
 
 def panel_kernel(
@@ -694,14 +576,781 @@
             dma((3,)),
         ],
         compiler_params=pltpu.CompilerParams(
-            collective_id=1, has_side_effects=True, vmem_limit_bytes=40 * 1024 * 1024
+            collective_id=2, has_side_effects=True, vmem_limit_bytes=40 * 1024 * 1024
         ),
     )(dense, separator, inverses, pivots)
 
 
+def general(separator, left_factor, right_factor, owners, spots, pivot_order, panel_inverses):
+    destination = owners[:, 0]
+    counter = jnp.arange(OWNERS)
+    same = destination[:, None] == destination[None, :]
+    rank = jnp.sum(same & (counter[None, :] < counter[:, None]), axis=1)
+    named = (destination[None, :] == jnp.arange(2 * OWNERS)[:, None] % OWNERS) & (
+        rank[None, :] == jnp.arange(2 * OWNERS)[:, None] // OWNERS
+    )
+    index = jnp.sum(jnp.where(named, counter[None, :], 0), axis=1).astype(I32)
+    placed = jnp.where(jnp.any(named, axis=1), jnp.sum(jnp.where(named, spots[None, :], 0), axis=1), 64)
+    table = jnp.broadcast_to(placed.astype(I32)[None, :], (8, 2 * OWNERS))
+    recv, tables = exchange(index, table, left_factor, right_factor)
+    col = lax.axis_index("pcol")
+    me = lax.axis_index("prow") * GRID + col
+    arrived = lax.dynamic_index_in_dim(tables[:, 0, :].reshape(OWNERS, 2, OWNERS), me, 2, keepdims=False)
+    spot = arrived.reshape(2 * OWNERS)
+    i, j = spot // 8, spot % 8
+    inside = jnp.where(j < 4, (i // 2) * 16 + j * 2 + i % 2, (2 * (j - 4) + 1) * 8 + i)
+    slots = jnp.where(spot < 64, jnp.where(col == 0, inside, j * 8 + i), 64)
+    dense = scatter(slots, recv.reshape(2 * OWNERS, BLOCK, BLOCK))
+    return panel(dense.reshape(8, 1024, BLOCK), separator, panel_inverses, pivot_order[:, None])
+
+
+SCRATCH = (
+    ("mains", "each", lambda n: ((2 * GRID, GRID, n, BLOCK), F32)),
+    ("dense", "each", lambda n: ((OWNERS, n, BLOCK), F32)),
+    ("relay", "each", lambda n: ((2, 8, n, BLOCK), F32)),
+    ("comb", "each", lambda n: ((2, 8, n, BLOCK), F32)),
+    ("plain", "each", lambda n: ((2, 8, n, BLOCK), F32)),
+    ("piece", "each", lambda n: ((8, 8, n, BLOCK), F32)),
+    ("top", "each", lambda n: ((8, 4, n, BLOCK), F32)),
+    ("left", "each", lambda n: ((LAYERS, 8, n, BLOCK), F32)),
+    ("low", "each", lambda n: ((8 * n, 512), F32)),
+    ("low_hi", "each", lambda n: ((8 * n, 512), BF16)),
+    ("low_lo", "each", lambda n: ((8 * n, 512), BF16)),
+    ("result", "each", lambda n: ((8, n, 1024), F32)),
+    ("ring", "one", ((GRID, BLOCK, BLOCK), F32)),
+    ("out_buf", "one", ((OWNERS, BLOCK, BLOCK), F32)),
+    ("table_buf", "one", ((GRID, GRID, 8, BLOCK), I32)),
+    ("peak_buf", "one", ((LAYERS, 8, BLOCK), I32)),
+    ("index_buf", "one", ((8, BLOCK), I32)),
+    ("sorted_buf", "one", ((8, BLOCK), I32)),
+    ("running", "one", ((2 * OWNERS, max(THINS), BLOCK), F32)),
+    ("sep_buf", "one", ((2, 1024, BLOCK), F32)),
+    ("up", "one", ((512, 1024), F32)),
+    ("up_hi", "one", ((512, 1024), BF16)),
+    ("up_lo", "one", ((512, 1024), BF16)),
+    ("inv_lp", "one", ((512, 512), BF16)),
+    ("inv_u", "one", ((512, 512), BF16)),
+    ("perm", "one", ((512, 512), BF16)),
+    ("index_mem", "smem", ((8, BLOCK), I32)),
+    ("sorted_mem", "smem", ((8, BLOCK), I32)),
+    ("a_sem", "sem", (2, SLICES, OWNERS)),
+    ("p_sem", "sem", (2, LAYERS)),
+    ("z_sem", "sem", (2, 2, 2, 5)),
+    ("y_sem", "sem", (2, SLICES, LAYERS)),
+    ("c_sem", "sem", (2, SLICES, LAYERS)),
+    ("ty_sem", "sem", (2, LAYERS)),
+    ("tc_sem", "sem", (2, LAYERS)),
+    ("mem_sem", "sem", (2,)),
+    ("sep_sem", "sem", (6,)),
+    ("rs_sem", "sem", (2, SLICES, 6)),
+    ("ag_sem", "sem", (2, SLICES, 2, 2)),
+    ("fw_sem", "sem", (2, SLICES, 2)),
+    ("top_sem", "sem", (3, SLICES, 2)),
+    ("tx_sem", "sem", (2, SLICES, 2, LAYERS)),
+    ("ly_sem", "sem", (SLICES, 1 + GRID)),
+    ("lx_sem", "sem", (2, SLICES, LAYERS)),
+    ("lc_sem", "sem", (2, SLICES, LAYERS)),
+    ("out_sem", "sem", (SLICES, 8)),
+)
+
+
+def scratch_shapes():
+    shapes = []
+    for _, kind, what in SCRATCH:
+        if kind == "each":
+            shapes += [pltpu.VMEM(*what(n)) for n in THINS]
+        elif kind == "one":
+            shapes.append(pltpu.VMEM(*what))
+        elif kind == "smem":
+            shapes.append(pltpu.SMEM(*what))
+        else:
+            shapes.append(pltpu.SemaphoreType.DMA(what))
+    return shapes
+
+
+class Scratch:
+    def __init__(self, refs):
+        at = 0
+        for name, kind, _ in SCRATCH:
+            if kind == "each":
+                setattr(self, name, refs[at : at + SLICES])
+                at += SLICES
+            else:
+                setattr(self, name, refs[at])
+                at += 1
+
+
+def fused_kernel(
+    owners_ref, spots_ref, left_ref, right_ref, sep_ref, inv_ref, pivot_ref, out_ref, peak_ref, *refs
+):
+    b = Scratch(refs)
+    layer, row, col = lax.axis_index("layer"), lax.axis_index("prow"), lax.axis_index("pcol")
+    me = row * GRID + col
+    core = col % 2
+    nxt, prv, opp = (layer + 1) % LAYERS, (layer + 3) % LAYERS, (layer + 2) % LAYERS
+    edge = col == 0
+    inner = jnp.logical_not(edge)
+    head = row == 0
+    up_row, down_row = (row + 1) % GRID, (row + GRID - 1) % GRID
+    to_nxt, to_prv = (nxt, row, col), (prv, row, col)
+    sibling = (layer, row, col + 1 - 2 * core)
+
+    def remote(src, dst, sems, device):
+        return pltpu.make_async_remote_copy(
+            src_ref=src, dst_ref=dst, send_sem=sems[0], recv_sem=sems[1], device_id=device, device_id_type=MESH
+        )
+
+    def pair(sem, *at):
+        return sem.at[(0, *at)], sem.at[(1, *at)]
+
+    def place(k):
+        return (row + k % GRID) % GRID, (col + k // GRID) % GRID
+
+    def other(k):
+        return ((layer + k) % LAYERS, row, col)
+
+    def column(q, h):
+        return jnp.where(edge, 4 + q, 2 * q + h)
+
+    barrier = pltpu.get_barrier_semaphore()
+
+    def greet(k, carry):
+        r, c = place(k)
+        pl.semaphore_signal(barrier, inc=1, device_id=(layer, r, c), device_id_type=MESH)
+        return carry
+
+    lax.fori_loop(1, OWNERS, greet, 0)
+    for k in range(1, LAYERS):
+        pl.semaphore_signal(barrier, inc=1, device_id=other(k), device_id_type=MESH)
+
+    def sep_whole(h):
+        return pltpu.make_async_copy(
+            sep_ref.at[:, pl.ds(pl.multiple_of(column(layer, h) * BLOCK, BLOCK), BLOCK)],
+            b.sep_buf.at[h],
+            b.sep_sem.at[h],
+        )
+
+    def sep_edge(j):
+        return pltpu.make_async_copy(
+            sep_ref.at[pl.ds(pl.multiple_of(layer * 256, 256), 256), pl.ds(j * BLOCK, BLOCK)],
+            b.sep_buf.at[0, pl.ds(j * 256, 256)],
+            b.sep_sem.at[2 + j],
+        )
+
+    sep_whole(1).start()
+
+    @pl.when(inner)
+    def _():
+        sep_whole(0).start()
+
+    @pl.when(edge)
+    def _():
+        for j in range(4):
+            sep_edge(j).start()
+
+    lane = lax.broadcasted_iota(I32, (OWNERS, BLOCK), 1)
+    line = lax.broadcasted_iota(I32, (OWNERS, BLOCK), 0)
+    lane_row = lax.broadcasted_iota(I32, (1, BLOCK), 1)
+    owner_all = jnp.broadcast_to(jnp.concatenate([owners_ref[...], spots_ref[...]], axis=1), (BLOCK, BLOCK))
+    owner_row, both = owner_all[:OWNERS], owner_all.T
+    owner_col, spot_col = both[:OWNERS], both[OWNERS:]
+    rank = wide(across(jnp.where((owner_row == owner_col) & (lane < line), 1, 0)))
+    hit = (owner_col == lane) & (rank == 0)
+    index_row = down(jnp.where(hit, line, 0))
+    spot_row = down(jnp.where(hit, spot_col, 0))
+    hits = down(jnp.where(hit, 1, 0))
+    second = rank == 1
+    count_row = down(jnp.where(second, 1, 0))
+    chosen = jnp.min(jnp.where(second, line, OWNERS), axis=0, keepdims=True)
+    pick = line == chosen
+    code_row = down(jnp.where(pick, owner_col * 64 + spot_col, 0))
+    chosen_row = down(jnp.where(pick, line, 0))
+    index_row = jnp.where(lane_row < OWNERS, index_row, chosen_row)
+    spot_row = jnp.where(hits > 0, spot_row, 64)
+    code_row = jnp.where(count_row > 0, code_row, -1)
+    table_row = jnp.where(lane_row < OWNERS, spot_row, jnp.where(lane_row == OWNERS, code_row, count_row))
+    b.table_buf[row, col] = jnp.broadcast_to(table_row, (8, BLOCK))
+    b.index_buf[...] = jnp.broadcast_to(index_row, (8, BLOCK))
+    to_mem = pltpu.make_async_copy(b.index_buf, b.index_mem, b.mem_sem.at[0])
+    to_mem.start()
+    to_mem.wait()
+
+    def multiply(u):
+        return dot(left_ref[u], right_ref[u])
+
+    def product(k):
+        r, c = place(k)
+        b.out_buf[k] = multiply(b.index_mem[0, r * GRID + c])
+
+    def slice_copy(k, s):
+        r, c = place(k)
+        return remote(
+            b.out_buf.at[k, pl.ds(STARTS[s], THINS[s])], b.mains[s].at[row, col], pair(b.a_sem, s, k), (layer, r, c)
+        )
+
+    def peak_copy(k):
+        return remote(b.peak_buf.at[0], b.peak_buf.at[k], pair(b.p_sem, k), other(k))
+
+    def ring_copies(h):
+        copies = []
+        for d in range(2 if h <= 3 else 1):
+            source = (row + GRID - h + 1) % GRID if d == 0 else (row + h - 1) % GRID
+            device = (layer, (up_row if d == 0 else down_row), col)
+            block, table = b.ring.at[source], b.table_buf.at[source, col]
+            copies.append(remote(block, block, pair(b.z_sem, 0, d, h), device))
+            copies.append(remote(table, table, pair(b.z_sem, 1, d, h), device))
+        return copies
+
+    def row_copy(s, k):
+        return remote(
+            b.ring.at[:, pl.ds(STARTS[s], THINS[s])],
+            b.mains[s].at[pl.ds(GRID, GRID), col],
+            pair(b.y_sem, s, k),
+            (layer, row, (col + 2 * k) % GRID),
+        )
+
+    def core_copy(s, k):
+        part = b.mains[s].at[pl.ds(GRID, GRID), (col + GRID - 2 * k) % GRID]
+        return remote(part, part, pair(b.c_sem, s, k), sibling)
+
+    def row_table(k):
+        part = b.table_buf.at[:, col]
+        return remote(part, part, pair(b.ty_sem, k), (layer, row, (col + 2 * k) % GRID))
+
+    def core_table(k):
+        part = b.table_buf.at[:, (col + GRID - 2 * k) % GRID]
+        return remote(part, part, pair(b.tc_sem, k), sibling)
+
+    def early(k, carry):
+        product(k)
+        return carry
+
+    b.ring[row] = multiply(b.index_mem[0, OWNERS])
+    lax.fori_loop(1, 1 + EARLY, early, 0, unroll=4)
+    pl.semaphore_wait(barrier, OWNERS - 1 + LAYERS - 1)
+
+    def first_slice(k, carry):
+        slice_copy(k, 0).start()
+        product(k + EARLY)
+        return carry
+
+    def send_slice(s, first=1):
+        def send(k, carry):
+            slice_copy(k, s).start()
+            return carry
+
+        lax.fori_loop(first, OWNERS, send, 0)
+
+    for op in ring_copies(1):
+        op.start()
+    lax.fori_loop(1, 9, first_slice, 0)
+    for h in range(1, 4):
+        for op in ring_copies(h):
+            op.wait_recv()
+        for op in ring_copies(h + 1):
+            op.start()
+        lax.fori_loop(1 + 8 * h, 9 + 8 * h, first_slice, 0)
+    for op in ring_copies(4):
+        op.wait_recv()
+    for k in (1, 3, 2):
+        row_table(k).start()
+    core_table(0).start()
+    for s in range(SLICES):
+        for k in (1, 3, 2):
+            row_copy(s, k).start()
+        for r in range(GRID):
+            b.mains[s][GRID + r, col] = b.ring[r, pl.ds(STARTS[s], THINS[s])]
+        core_copy(s, 0).start()
+    lax.fori_loop(33, OWNERS - EARLY, first_slice, 0)
+    send_slice(0, OWNERS - EARLY)
+    own = multiply(b.index_mem[0, me])
+    for s in range(SLICES):
+        b.mains[s][row, col] = own[STARTS[s] : STARTS[s] + THINS[s]]
+    for s in range(1, AHEAD):
+        send_slice(s)
+
+    inv = inv_ref[...].astype(F32)
+    rows_at = lax.broadcasted_iota(I32, (512, 512), 0)
+    cols_at = lax.broadcasted_iota(I32, (512, 512), 1)
+    lower_inverse = jnp.where(rows_at > cols_at, inv, jnp.where(rows_at == cols_at, 1.0, 0.0)).astype(BF16)
+    b.inv_u[...] = jnp.where(rows_at <= cols_at, inv, 0.0).astype(BF16)
+    for s in range(SLICES):
+        n = 4 * THINS[s]
+        at = lax.broadcasted_iota(I32, (n, 512), 0)
+        source = (at // THINS[s]) * BLOCK + STARTS[s] + at % THINS[s]
+        b.perm[pl.ds(4 * STARTS[s], n)] = jnp.where(pivot_ref[...] == source, 1.0, 0.0).astype(BF16)
+    b.inv_lp[...] = lax.dot_general(
+        lower_inverse, b.perm[...], (((1,), (1,)), ((), ())), preferred_element_type=F32
+    ).astype(BF16)
+
+    for k in (1, 3, 2):
+        row_table(k).wait_recv()
+        core_table(k).start()
+    for k in range(LAYERS):
+        core_table(k).wait_recv()
+    tables = b.table_buf[...].reshape(OWNERS, 8, BLOCK)
+    b.peak_buf[0] = jnp.max(tables, axis=0)
+    for k in range(1, LAYERS):
+        peak_copy(k).start()
+    tables = tables[:, 0, :]
+    mine = across(jnp.where(lane == me, tables, 0))
+    code = across(jnp.where(lane == OWNERS, tables, 0))
+    extra = jnp.where((code >= 0) & ((code >> 6) == me), code & 63, 64)
+    spot = jnp.concatenate([mine, extra], axis=0)
+    i, j = spot >> 3, spot & 7
+    inside = jnp.where(j < 4, (i >> 1) * 16 + j * 2 + (i & 1), (2 * (j - 4) + 1) * 8 + i)
+    slot_col = wide(jnp.where(spot < 64, jnp.where(edge, inside, j * 8 + i), 64))
+    slot_row = slot_col.T
+    line2 = lax.broadcasted_iota(I32, (BLOCK, BLOCK), 0)
+    lane2 = lax.broadcasted_iota(I32, (BLOCK, BLOCK), 1)
+    ahead = (slot_row < slot_col) | ((slot_row == slot_col) & (lane2 < line2))
+    rank2 = wide(across(jnp.where(ahead, 1, 0)))
+    order_row = down(jnp.where(rank2 == lane2, line2, 0))
+    slots_row = down(jnp.where(rank2 == lane2, slot_col, 0))
+    before_row = down(jnp.where(rank2 == lane2 - 1, slot_col, 0))
+    same_row = jnp.where((slots_row == before_row) & (lane_row > 0), 1, 0)
+    last_row = jnp.maximum(down(jnp.where(slot_col <= lane2, 1, 0)) - 1, 0)
+    filled_row = jnp.where(down(jnp.where(slot_col == lane2, 1, 0)) > 0, 1, 0)
+    b.sorted_buf[0:1] = order_row
+    b.sorted_buf[1:2] = same_row
+    b.sorted_buf[2:3] = last_row
+    b.sorted_buf[3:4] = filled_row
+    b.sorted_buf[4:8] = jnp.zeros((4, BLOCK), I32)
+    to_sorted = pltpu.make_async_copy(b.sorted_buf, b.sorted_mem, b.mem_sem.at[1])
+    to_sorted.start()
+    to_sorted.wait()
+
+    def spread_extras(s):
+        for k in (1, 3, 2):
+            row_copy(s, k).wait_recv()
+            core_copy(s, k).start()
+
+    def add_up(s):
+        thin = pl.ds(0, THINS[s])
+
+        def run(k, total):
+            e = b.sorted_mem[0, k]
+            total = b.mains[s][e >> 3, e & 7] + jnp.where(b.sorted_mem[1, k] == 1, total, 0.0)
+            b.running[k, thin] = total
+            return total
+
+        lax.fori_loop(0, 2 * OWNERS, run, jnp.zeros((THINS[s], BLOCK), F32), unroll=8)
+
+        def settle(k, carry):
+            value = b.running[b.sorted_mem[2, k], thin]
+            b.dense[s][k] = jnp.where(b.sorted_mem[3, k] == 1, value, 0.0)
+            return carry
+
+        lax.fori_loop(0, OWNERS, settle, 0, unroll=8)
+
+    def strip(s, q):
+        return b.dense[s].at[pl.ds(pl.multiple_of(8 * q, 8), 8)]
+
+    def relay_out(s):
+        return [
+            remote(strip(s, 2 * opp), b.relay[s].at[0], pair(b.rs_sem, s, 0), to_nxt),
+            remote(strip(s, 2 * opp + 1), b.relay[s].at[1], pair(b.rs_sem, s, 1), to_prv),
+        ]
+
+    def plain_out(s):
+        return [
+            remote(strip(s, 2 * prv), b.plain[s].at[0], pair(b.rs_sem, s, 2), to_prv),
+            remote(strip(s, 2 * nxt + 1), b.plain[s].at[1], pair(b.rs_sem, s, 3), to_nxt),
+        ]
+
+    def comb_out(s):
+        return [
+            remote(b.relay[s].at[0], b.comb[s].at[0], pair(b.rs_sem, s, 4), to_nxt),
+            remote(b.relay[s].at[1], b.comb[s].at[1], pair(b.rs_sem, s, 5), to_prv),
+        ]
+
+    def combine(s):
+        relays, combs = relay_out(s), comb_out(s)
+        for h, q in ((0, 2 * nxt), (1, 2 * prv + 1)):
+            relays[h].wait_recv()
+            b.relay[s][h] += b.dense[s][pl.ds(pl.multiple_of(8 * q, 8), 8)]
+            combs[h].start()
+
+    def gather_copy(s, h, d):
+        part = b.piece[s].at[column(layer, h)]
+        return remote(part, part, pair(b.ag_sem, s, h, d), to_nxt if d == 0 else to_prv)
+
+    def gather_pass(s, d):
+        part = b.piece[s].at[column(prv if d == 0 else nxt, d)]
+        return remote(part, part, pair(b.fw_sem, s, d), to_nxt if d == 0 else to_prv)
+
+    def top_copy(s, h, d):
+        part = b.top[s].at[column(layer, h)]
+        device = (layer, up_row if d == 0 else down_row, col)
+        return remote(part, part, (b.top_sem.at[d, s, h], b.top_sem.at[2, s, h]), device)
+
+    def top_other(s, h, k):
+        part = b.top[s].at[column(layer, h)]
+        return remote(part, part, pair(b.tx_sem, s, h, k), other(k))
+
+    onward = jnp.logical_and(row >= 1, row <= 3)
+    backward = row >= 6
+
+    def left_part(s, q, c):
+        return b.left[s].at[q, pl.ds(pl.multiple_of((c % 2) * 4, 4), 4)]
+
+    def left_row(s, k):
+        c = (col + k) % GRID
+        part = left_part(s, layer, c)
+        return remote(part, part, (b.ly_sem.at[s, k], b.ly_sem.at[s, 0]), (layer, row, c))
+
+    def left_row_wait(s):
+        part = left_part(s, layer, col)
+        op = remote(part, part, (b.ly_sem.at[s, 1], b.ly_sem.at[s, 0]), (layer, row, (col + 1) % GRID))
+        op.wait_recv()
+
+    def left_other(s, k):
+        part = left_part(s, layer, col)
+        return remote(part, part, pair(b.lx_sem, s, k), other(k))
+
+    def left_core(s, k):
+        part = left_part(s, (layer + k) % LAYERS, col)
+        return remote(part, part, pair(b.lc_sem, s, k), sibling)
+
+    def halves(action):
+        action(1)
+        pl.when(inner)(lambda: action(0))
+
+    def reduce(s):
+        plains, combs = plain_out(s), comb_out(s)
+        n = THINS[s]
+
+        def value(h, k):
+            return b.sep_buf[h, pl.ds(k * BLOCK + STARTS[s], n)] - (
+                b.dense[s][8 * (2 * layer + h) + k] + b.plain[s][h, k] + b.comb[s][h, k]
+            )
+
+        for h in range(2):
+            plains[h].wait_recv()
+            combs[h].wait_recv()
+        for k in range(8):
+            b.piece[s][column(layer, 1), k] = value(1, k)
+
+        @pl.when(inner)
+        def _():
+            for k in range(8):
+                b.piece[s][2 * layer, k] = value(0, k)
+
+        @pl.when(edge)
+        def _():
+            for k in range(8):
+                b.left[s][layer, k] = value(0, k)
+            for k in (2, 6, 3, 7, 4, 5, 1):
+                left_row(s, k).start()
+
+        @pl.when(head)
+        def _():
+            def keep(h):
+                b.top[s][column(layer, h)] = b.piece[s][column(layer, h), pl.ds(0, 4)]
+
+            halves(keep)
+
+        @pl.when(inner)
+        def _():
+            gather_copy(s, 0, 0).start()
+            gather_copy(s, 0, 1).start()
+
+        gather_copy(s, 1, 1).start()
+        gather_copy(s, 1, 0).start()
+
+    def top_out(s):
+        @pl.when(head)
+        def _():
+            def send(h):
+                top_copy(s, h, 0).start()
+                top_copy(s, h, 1).start()
+
+            halves(send)
+
+    def pass_top(s):
+        @pl.when(jnp.logical_not(head))
+        def _():
+            def onwards(h):
+                top_copy(s, h, 0).wait_recv()
+
+                @pl.when(onward)
+                def _():
+                    top_copy(s, h, 0).start()
+
+                @pl.when(backward)
+                def _():
+                    top_copy(s, h, 1).start()
+
+            halves(onwards)
+
+        def to_others(h):
+            for k in (1, 3, 2):
+                top_other(s, h, k).start()
+
+        halves(to_others)
+
+    def pass_on(s):
+        @pl.when(inner)
+        def _():
+            left_row_wait(s)
+
+        for k in (1, 3, 2):
+            left_other(s, k).start()
+
+        @pl.when(col != 1)
+        def _():
+            left_core(s, 0).start()
+
+        @pl.when(inner)
+        def _():
+            gather_copy(s, 0, 0).wait_recv()
+            gather_pass(s, 0).start()
+
+        gather_copy(s, 1, 1).wait_recv()
+        gather_pass(s, 1).start()
+        for k in (1, 3, 2):
+            left_other(s, k).wait_recv()
+            left_core(s, LAYERS - k).start()
+
+    def lower_panel(s):
+        n = THINS[s]
+
+        @pl.when(inner)
+        def _():
+            left_core(s, 0).wait_recv()
+
+        for k in range(1, LAYERS):
+            left_core(s, k).wait_recv()
+        rows = []
+        for q in range(LAYERS):
+            for i2 in range(2):
+                rows.append(jnp.concatenate([b.left[s][q, 2 * j + i2] for j in range(4)], axis=1))
+        hi, lo = split(jnp.concatenate(rows, axis=0))
+        lower = dot(hi, b.inv_u[...]) + dot(lo, b.inv_u[...])
+        b.low[s][...] = lower
+        hi, lo = split(lower)
+        b.low_hi[s][...] = hi
+        b.low_lo[s][...] = lo
+
+    def upper_panel(s):
+        n = THINS[s]
+
+        def arrived(h):
+            for k in (1, 3, 2):
+                top_other(s, h, k).wait_recv()
+
+        halves(arrived)
+
+        def add(c, carry):
+            at = pl.ds(pl.multiple_of(c * 256, 256), 256)
+            strips = [b.top[s][2 * c + h].reshape(4 * n, BLOCK) for h in range(2)]
+            hi, lo = split(jnp.concatenate(strips, axis=1))
+            inv = b.inv_lp[:, pl.ds(4 * STARTS[s], 4 * n)]
+            term = dot(inv, hi) + dot(inv, lo)
+            if s == 0:
+                b.up[:, at] = term
+            elif s < SLICES - 1:
+                b.up[:, at] += term
+            else:
+                total = b.up[:, at] + term
+                b.up[:, at] = total
+                hi, lo = split(total)
+                b.up_hi[:, at] = hi
+                b.up_lo[:, at] = lo
+            return carry
+
+        lax.fori_loop(0, 4, add, 0)
+
+    spread_extras(0)
+    for s in range(SLICES):
+        for k in range(LAYERS):
+            core_copy(s, k).wait_recv()
+
+        def slice_wait(k, carry):
+            slice_copy(k, s).wait_recv()
+            return carry
+
+        lax.fori_loop(1, OWNERS, slice_wait, 0)
+        add_up(s)
+        for op in relay_out(s) + plain_out(s):
+            op.start()
+        if s == 0:
+
+            @pl.when(inner)
+            def _():
+                sep_whole(0).wait()
+
+            @pl.when(edge)
+            def _():
+                for j in range(4):
+                    sep_edge(j).wait()
+
+            sep_whole(1).wait()
+        if s + AHEAD < SLICES:
+            send_slice(s + AHEAD)
+        if s + 1 < SLICES:
+            spread_extras(s + 1)
+        last = s == SLICES - 1
+        if last:
+            for t in range(s):
+                top_out(t)
+        if s >= 1:
+            pass_on(s - 1)
+        combine(s)
+        if last:
+            for t in range(s):
+                pass_top(t)
+        reduce(s)
+        if last:
+            top_out(s)
+        if s >= 2:
+            lower_panel(s - 2)
+    pass_on(SLICES - 1)
+    pass_top(SLICES - 1)
+    lower_panel(SLICES - 2)
+    for s in range(SLICES - 1):
+        upper_panel(s)
+    lower_panel(SLICES - 1)
+    upper_panel(SLICES - 1)
+
+    def out_copy(s):
+        return [
+            pltpu.make_async_copy(
+                b.result[s].at[i], out_ref.at[pl.ds(i * BLOCK + STARTS[s], THINS[s])], b.out_sem.at[s, i]
+            )
+            for i in range(8)
+        ]
+
+    @pl.when(jnp.logical_and(edge, head))
+    def _():
+        rows = []
+        for s in range(SLICES):
+            for q in range(2):
+                for i2 in range(2):
+                    rows.append(jnp.concatenate([b.left[s][q, 2 * j + i2] for j in range(4)], axis=1))
+        whole = jnp.concatenate(rows, axis=0)
+        first, _ = split(whole)
+        second, third = split(whole - first.astype(F32))
+        order = b.perm[...].astype(F32).T.astype(BF16)
+        b.up[:, 0:512] = dot(order, first) + dot(order, second) + dot(order, third)
+
+    for s in range(SLICES):
+        n = THINS[s]
+
+        @pl.when(inner)
+        def _():
+            gather_copy(s, 0, 1).wait_recv()
+            gather_pass(s, 0).wait_recv()
+
+        gather_copy(s, 1, 0).wait_recv()
+        gather_pass(s, 1).wait_recv()
+
+        def trail(c, carry):
+            at = pl.ds(pl.multiple_of(c * 256, 256), 256)
+            hi, u_hi = b.low_hi[s][...], b.up_hi[:, at]
+            change = dot(hi, u_hi) + (dot(b.low_lo[s][...], u_hi) + dot(hi, b.up_lo[:, at]))
+            pieces = [b.piece[s][2 * c + h].reshape(8 * n, BLOCK) for h in range(2)]
+            b.result[s][:, :, at] = (jnp.concatenate(pieces, axis=1) - change).reshape(8, n, 256)
+
+            @pl.when(head)
+            def _():
+                for i in range(4):
+                    b.result[s][i, :, at] = b.up[pl.ds(i * BLOCK + STARTS[s], n), at]
+
+            return carry
+
+        lax.fori_loop(0, 4, trail, 0)
+
+        @pl.when(edge)
+        def _():
+            lower = b.low[s][...].reshape(8, n, 512)
+            b.result[s][4:8, :, 0:512] = lower[4:8]
+
+            @pl.when(jnp.logical_not(head))
+            def _():
+                b.result[s][0:4, :, 0:512] = lower[0:4]
+
+        for op in out_copy(s):
+            op.start()
+
+    for s in range(SLICES):
+        def sent(k, carry):
+            slice_copy(k, s).wait_send()
+            return carry
+
+        lax.fori_loop(1, OWNERS, sent, 0)
+        for op in relay_out(s) + plain_out(s) + comb_out(s):
+            op.wait_send()
+        for k in range(1, LAYERS):
+            row_copy(s, k).wait_send()
+            left_other(s, k).wait_send()
+            left_core(s, k).wait_send()
+        for k in range(LAYERS):
+            core_copy(s, k).wait_send()
+
+        @pl.when(col != 1)
+        def _():
+            left_core(s, 0).wait_send()
+
+        @pl.when(edge)
+        def _():
+            for k in range(1, GRID):
+                left_row(s, k).wait_send()
+
+        def gone(h):
+            @pl.when(jnp.logical_or(head, onward))
+            def _():
+                top_copy(s, h, 0).wait_send()
+
+            @pl.when(jnp.logical_or(head, backward))
+            def _():
+                top_copy(s, h, 1).wait_send()
+
+            for k in range(1, LAYERS):
+                top_other(s, h, k).wait_send()
+            for d in range(2):
+                gather_copy(s, h, d).wait_send()
+            gather_pass(s, h).wait_send()
+
+        halves(gone)
+    for h in range(1, 5):
+        for op in ring_copies(h):
+            op.wait_send()
+    for k in range(1, LAYERS):
+        peak_copy(k).wait()
+        row_table(k).wait_send()
+    for k in range(LAYERS):
+        core_table(k).wait_send()
+    peak_ref[...] = jnp.max(b.peak_buf[...], axis=0)
+    for s in range(SLICES):
+        for op in out_copy(s):
+            op.wait()
+
+
+def fused(owners, spots, left, right, separator, inverses, pivots):
+    vmem = pl.BlockSpec(memory_space=pltpu.VMEM)
+    hbm = pl.BlockSpec(memory_space=pl.ANY)
+    return pl.pallas_call(
+        fused_kernel,
+        out_shape=(jax.ShapeDtypeStruct((8 * BLOCK, 1024), F32), jax.ShapeDtypeStruct((8, BLOCK), I32)),
+        in_specs=[vmem, vmem, vmem, vmem, hbm, vmem, vmem],
+        out_specs=(hbm, vmem),
+        scratch_shapes=scratch_shapes(),
+        compiler_params=pltpu.CompilerParams(
+            collective_id=0, has_side_effects=True, vmem_limit_bytes=56 * 1024 * 1024
+        ),
+    )(owners, spots, left, right, separator, inverses, pivots)
+
+
 def per_device(separator, left_factor, right_factor, owners, spots, pivot_order, panel_inverses):
-    dense = local_sum(left_factor, right_factor, owners, spots)
-    return panel(dense.reshape(8, 1024, BLOCK), separator, panel_inverses, pivot_order[:, None])
+    result, peak = fused(
+        owners[:, 0][None, :], spots[None, :], left_factor, right_factor, separator, panel_inverses, pivot_order[None, :]
+    )
+    return lax.cond(
+        peak[0, BLOCK - 1] > 1,
+        lambda: general(separator, left_factor, right_factor, owners, spots, pivot_order, panel_inverses),
+        lambda: result,
+    )
 
 
 def solution(mesh):

time: 282 us -> 218 us (0.77)
  Pallas kernels: 247 us -> 211 us
  between operations: 13.7 us -> 0.75 us
  local copies, waits for them, and re-layouts: 15.1 us -> 6.08 us
  other arithmetic: 4.26 us -> 0 us
    pallas_call x3 -> x1, Pallas kernels: 247 us -> 211 us  [fused(): pl.pallas_call(fused_kernel, out_shape=(jax.ShapeDtypeStruct((8 * BLOCK,...]
    unnamed x13, local copies, waits for them, and re-layouts: 10.9 us -> 4.81 us
  transfers between devices with their start and end apart: 1 -> 0, of which waited for: 0 -> 0; matrix products, arithmetic and copies ran while one was open for 2% -> 0% of each run, Pallas kernels for 45% -> 0%
where the time goes in v4:
time: 218 us
  Pallas kernels  211 us (97%)
  local copies, waits for them, and re-layouts  6.08 us (3%)
    pallas_call x1, Pallas kernels, fused(): pl.pallas_call(fused_kernel, out_shape=(jax.ShapeDtypeStruct((8 * BLOCK,...  211 us
    unnamed x13, local copies, waits for them, and re-layouts  4.81 us

profile of v4, /device:TPU:144, one launch (start us, length us, event | category | flops | bytes accessed | tf_op | source)
XLA Modules:
  0.0 217.8 jit_solution(1687014544513105298)
XLA Ops:
  0.0 0.0 copy-start.4
  0.0 0.0 copy-start.5
  0.0 0.0 copy-start.6
  0.0 0.0 copy-start.7
  0.0 0.0 copy-start.8
  0.0 0.0 copy-start.9
  0.0 210.8 %shard_map.75 = (f32[1024,1024]{1,0:T(8,128)}, s32[8,128]{1,0:T(8,128)}) custom-call(s32[1,64]{1,0:T(1,128)} %bitcast.12, s32[1,64]{1,0:T(1,128)} %bitcast.16, bf16[64,128,128]{2,1,0:T(8,128)(2,1)} %left_ref.1, bf16[64,128,128]{2,1,0:T(8,128)(2,1)} %right_ref.1, f32[1024,1024]{1,0:T(8,128)} %sep_ref.1, bf16[512,512]{1,0:T(8,128)(2,1)} %inv_ref.1, ...), custom_call_target="tpu_custom_call" | custom-call | tf_op jit(solution)/shard_map/pallas_call | solution.py:1333
  210.8 1.3 slice.6
  212.7 0.0 copy-done.4
  212.7 0.0 copy-done.5
  212.8 0.0 copy-done.6
  212.8 0.0 copy-done.7
  212.8 0.0 copy-done.8
  212.8 0.0 copy-done.9
  212.8 0.2 conditional.1
  213.0 4.8 %copy.19 = f32[1024,1024]{1,0:T(8,128)} copy(f32[1024,1024]{1,0:T(8,128)} %get-tuple-element.36) | data formatting | bytes 8388608
Async XLA Ops:
  0.0 212.7 %copy-start.4 = (bf16[64,128,128]{2,1,0:T(8,128)(2,1)S(1)}, bf16[64,128,128]{2,1,0:T(8,128)(2,1)}, u32[]{:S(2)}) copy-start(bf16[64,128,128]{2,1,0:T(8,128)(2,1)} %left_ref.1) | copy-start | bytes 6291460
  0.0 212.7 %copy-start.5 = (bf16[64,128,128]{2,1,0:T(8,128)(2,1)S(1)}, bf16[64,128,128]{2,1,0:T(8,128)(2,1)}, u32[]{:S(2)}) copy-start(bf16[64,128,128]{2,1,0:T(8,128)(2,1)} %right_ref.1) | copy-start | bytes 6291460
  0.0 212.7 %copy-start.6 = (bf16[512,512]{1,0:T(8,128)(2,1)S(1)}, bf16[512,512]{1,0:T(8,128)(2,1)}, u32[]{:S(2)}) copy-start(bf16[512,512]{1,0:T(8,128)(2,1)} %inv_ref.1) | copy-start | bytes 1572868
  0.0 212.8 %copy-start.7 = (s32[512]{0:T(512)S(1)}, s32[512]{0:T(512)}, u32[]{:S(2)}) copy-start(s32[512]{0:T(512)} %param.14) | copy-start | bytes 6148
  0.0 212.8 %copy-start.8 = (s32[64,1]{0,1:T(1,128)S(1)}, s32[64,1]{0,1:T(1,128)}, u32[]{:S(2)}) copy-start(s32[64,1]{0,1:T(1,128)} %param.12) | copy-start | bytes 772
  0.0 212.8 %copy-start.9 = (s32[64]{0:T(128)S(1)}, s32[64]{0:T(128)}, u32[]{:S(2)}) copy-start(s32[64]{0:T(128)} %param.13) | copy-start | bytes 772

commit v5 on v4

--- a/solution.py
+++ b/solution.py
@@ -1040,8 +1040,6 @@
         def _():
             for k in range(8):
                 b.left[s][layer, k] = value(0, k)
-            for k in (2, 6, 3, 7, 4, 5, 1):
-                left_row(s, k).start()
 
         @pl.when(head)
         def _():
@@ -1089,7 +1087,20 @@
 
         halves(to_others)
 
-    def pass_on(s):
+    def slice_sent(s):
+        def sent(k, carry):
+            slice_copy(k, s).wait_send()
+            return carry
+
+        lax.fori_loop(1, OWNERS, sent, 0)
+
+    def left_out(s):
+        @pl.when(edge)
+        def _():
+            for k in (2, 6, 3, 7, 4, 5, 1):
+                left_row(s, k).start()
+
+    def pass_left(s):
         @pl.when(inner)
         def _():
             left_row_wait(s)
@@ -1101,16 +1112,19 @@
         def _():
             left_core(s, 0).start()
 
-        @pl.when(inner)
-        def _():
-            gather_copy(s, 0, 0).wait_recv()
-            gather_pass(s, 0).start()
-
-        gather_copy(s, 1, 1).wait_recv()
-        gather_pass(s, 1).start()
+    def pass_core(s):
         for k in (1, 3, 2):
             left_other(s, k).wait_recv()
             left_core(s, LAYERS - k).start()
+
+    def pass_on(s):
+        @pl.when(inner)
+        def _():
+            gather_copy(s, 0, 0).wait_recv()
+            gather_pass(s, 0).start()
+
+        gather_copy(s, 1, 1).wait_recv()
+        gather_pass(s, 1).start()
 
     def lower_panel(s):
         n = THINS[s]
@@ -1194,22 +1208,31 @@
         if last:
             for t in range(s):
                 top_out(t)
+                left_out(t)
         if s >= 1:
             pass_on(s - 1)
         combine(s)
+        if s >= 1:
+            slice_sent(s - 1)
         if last:
             for t in range(s):
                 pass_top(t)
+            for t in range(s):
+                pass_left(t)
         reduce(s)
         if last:
             top_out(s)
-        if s >= 2:
-            lower_panel(s - 2)
+            left_out(s)
+    slice_sent(SLICES - 1)
+    pass_top(SLICES - 1)
+    for s in range(SLICES - 1):
+        pass_core(s)
     pass_on(SLICES - 1)
-    pass_top(SLICES - 1)
-    lower_panel(SLICES - 2)
+    pass_left(SLICES - 1)
     for s in range(SLICES - 1):
+        lower_panel(s)
         upper_panel(s)
+    pass_core(SLICES - 1)
     lower_panel(SLICES - 1)
     upper_panel(SLICES - 1)
 
@@ -1274,11 +1297,6 @@
             op.start()
 
     for s in range(SLICES):
-        def sent(k, carry):
-            slice_copy(k, s).wait_send()
-            return carry
-
-        lax.fori_loop(1, OWNERS, sent, 0)
         for op in relay_out(s) + plain_out(s) + comb_out(s):
             op.wait_send()
         for k in range(1, LAYERS):

time: 218 us -> 212 us (0.972)
  the two profiles are of different devices: /device:TPU:144 before, /device:TPU:9 now
where the time goes in v5:
time: 212 us
  Pallas kernels  205 us (97%)
  local copies, waits for them, and re-layouts  6.08 us (3%)
    pallas_call x1, Pallas kernels, fused(): pl.pallas_call(fused_kernel, out_shape=(jax.ShapeDtypeStruct((8 * BLOCK,...  205 us
    unnamed x13, local copies, waits for them, and re-layouts  4.81 us

profile of v5, /device:TPU:9, one launch (start us, length us, event | category | flops | bytes accessed | tf_op | source)
XLA Modules:
  0.0 212.2 jit_solution(14155648790989758969)
XLA Ops:
  0.0 0.0 copy-start.4
  0.0 0.0 copy-start.5
  0.0 0.0 copy-start.6
  0.0 0.0 copy-start.7
  0.0 0.0 copy-start.8
  0.0 0.0 copy-start.9
  0.0 205.2 %shard_map.75 = (f32[1024,1024]{1,0:T(8,128)}, s32[8,128]{1,0:T(8,128)}) custom-call(s32[1,64]{1,0:T(1,128)} %bitcast.12, s32[1,64]{1,0:T(1,128)} %bitcast.16, bf16[64,128,128]{2,1,0:T(8,128)(2,1)} %left_ref.1, bf16[64,128,128]{2,1,0:T(8,128)(2,1)} %right_ref.1, f32[1024,1024]{1,0:T(8,128)} %sep_ref.1, bf16[512,512]{1,0:T(8,128)(2,1)} %inv_ref.1, ...), custom_call_target="tpu_custom_call" | custom-call | tf_op jit(solution)/shard_map/pallas_call | solution.py:1351
  205.2 1.3 slice.6
  207.2 0.0 copy-done.4
  207.2 0.0 copy-done.5
  207.2 0.0 copy-done.6
  207.2 0.0 copy-done.7
  207.2 0.0 copy-done.8
  207.2 0.0 copy-done.9
  207.2 0.2 conditional.1
  207.5 4.8 %copy.19 = f32[1024,1024]{1,0:T(8,128)} copy(f32[1024,1024]{1,0:T(8,128)} %get-tuple-element.36) | data formatting | bytes 8388608
Async XLA Ops:
  0.0 207.2 %copy-start.4 = (bf16[64,128,128]{2,1,0:T(8,128)(2,1)S(1)}, bf16[64,128,128]{2,1,0:T(8,128)(2,1)}, u32[]{:S(2)}) copy-start(bf16[64,128,128]{2,1,0:T(8,128)(2,1)} %left_ref.1) | copy-start | bytes 6291460
  0.0 207.2 %copy-start.5 = (bf16[64,128,128]{2,1,0:T(8,128)(2,1)S(1)}, bf16[64,128,128]{2,1,0:T(8,128)(2,1)}, u32[]{:S(2)}) copy-start(bf16[64,128,128]{2,1,0:T(8,128)(2,1)} %right_ref.1) | copy-start | bytes 6291460
  0.0 207.2 %copy-start.6 = (bf16[512,512]{1,0:T(8,128)(2,1)S(1)}, bf16[512,512]{1,0:T(8,128)(2,1)}, u32[]{:S(2)}) copy-start(bf16[512,512]{1,0:T(8,128)(2,1)} %inv_ref.1) | copy-start | bytes 1572868
  0.0 207.2 %copy-start.7 = (s32[512]{0:T(512)S(1)}, s32[512]{0:T(512)}, u32[]{:S(2)}) copy-start(s32[512]{0:T(512)} %param.14) | copy-start | bytes 6148
  0.0 207.2 %copy-start.8 = (s32[64,1]{0,1:T(1,128)S(1)}, s32[64,1]{0,1:T(1,128)}, u32[]{:S(2)}) copy-start(s32[64,1]{0,1:T(1,128)} %param.12) | copy-start | bytes 772
  0.0 207.2 %copy-start.9 = (s32[64]{0:T(128)S(1)}, s32[64]{0:T(128)}, u32[]{:S(2)}) copy-start(s32[64]{0:T(128)} %param.13) | copy-start | bytes 772
